TPU v7x, 256 devices: a whole 4x4x8 slice. The times are simulated.
256 devices in a mesh: chan: 32 (over y_lo, z, core), tm: 8 (over y_hi, x).
Axes of the slice: x: 4, y: 4 (y_hi: 2, y_lo: 2; y = y_hi * 2 + y_lo), z: 8, core: 2. Of those that a mesh axis runs over, the one named last changes fastest.
Arguments:
- seismic: bfloat16 [3072, 32768], P('chan', 'tm'), may hold values from -180 to 180, as said below
- waveforms: float32 [32, 30, 300], P('chan'), may hold values from -0.5 to 1.5
- channel_list: int32 [32, 30], replicated, may hold values from 0 to 3071, as said below
- moveouts: int32 [32, 30], replicated, may hold values from 0 to 127
Outputs:
- stack: float32 [32, 32768], P('chan', 'tm')
- peaks: float32 [32], P('chan')
Inputs may be any that keep to these rules, and one draw needn't show every extreme that they name: `channel_list`: each template lists the three channels 3 s, 3 s + 1, 3 s + 2 of 10 stations s, station by station; no channel appears twice in the whole array; the first and the last channel are always listed. Of the groups of 96 consecutive channels, a quarter hold 60 listed channels, a quarter 3 * 10, and the other half 3 * 5; which groups is drawn. `seismic`: channels differ in gain, and the amplitude varies along time.
All inputs are finite; a program needn't handle non-finite values.
Results may differ from a plain program's by a relative error of at most 0.0029.
Values may be sent and summed in bfloat16 or wider, within the bound.
A program may use at most 128 MiB of HBM per device.

v0:
```python
import math

import jax
import jax.numpy as jnp
from jax import lax
from jax.sharding import PartitionSpec as P

MOVE = 128
TPL_CH = 30
TPL_DEV = 1
CAP = 60


eps_value = 1e-05
tile_width = 128


def from_behind(x, axis, by):
    size = lax.axis_size(axis)
    pairs = [(i, i + by) for i in range(size) if 0 <= i + by < size]
    return lax.ppermute(x, axis, pairs)


def normalize(waves):
    centered = waves - jnp.mean(waves, axis=-1, keepdims=True)
    factor = lax.rsqrt(
        jnp.mean(centered * centered, axis=-1, keepdims=True) + eps_value
    ) / math.sqrt(waves.shape[-1])
    return (centered * factor).astype(jnp.bfloat16)


def on_device(seismic, waveforms, channel_list, moveouts):
    group_index = lax.axis_index("chan")
    chan_count = seismic.shape[0]
    piece_len = seismic.shape[1]
    length = waveforms.shape[2]
    block_count = (length + MOVE + 253) // tile_width
    halo_len = (block_count - 1) * tile_width
    tail_rows = from_behind(seismic[:, :halo_len], "tm", -1)
    extended = jnp.concatenate([seismic, tail_rows], axis=1)
    every_wave = lax.all_gather(waveforms, "chan", axis=0, tiled=True)
    normed = normalize(every_wave)
    template_count = channel_list.shape[0]
    normed_flat = normed.reshape(-1, length)
    listed = channel_list.reshape(-1)
    pair_count = listed.shape[0]
    is_local = (listed // chan_count == group_index).astype(jnp.int32)
    ranking = jnp.cumsum(is_local) - is_local
    capacity = CAP
    matching = (
        (ranking[None, :] == jnp.arange(capacity, dtype=jnp.int32)[:, None])
        & (is_local[None, :] == 1)
    ).astype(jnp.int32)
    slot_pair = jnp.sum(matching * jnp.arange(pair_count, dtype=jnp.int32)[None, :], axis=1)
    slot_live = jnp.sum(matching, axis=1)
    slot_chan = jnp.clip(jnp.take(listed, slot_pair) - group_index * chan_count, 0, chan_count - 1)
    slot_move = jnp.take(moveouts.reshape(-1), slot_pair)
    slot_wave = jnp.take(normed_flat, slot_pair, axis=0) * slot_live[:, None].astype(jnp.bfloat16)
    slot_rows = jnp.take(extended, slot_chan, axis=0)
    owner_table = (
        (slot_pair[None, :] // TPL_CH == jnp.arange(template_count, dtype=jnp.int32)[:, None])
        & (slot_live[None, :] == 1)
    ).astype(jnp.float32)
    tile_count = piece_len // tile_width
    kernel_width = block_count * tile_width
    padded_width = kernel_width + tile_width
    position = jnp.arange(padded_width, dtype=jnp.int32)[None, :]
    source = position - slot_move[:, None]
    inside = (source >= 0) & (source < length)
    picked = jnp.take_along_axis(slot_wave, jnp.clip(source, 0, length - 1), axis=1)
    shifted = jnp.where(inside, picked, jnp.zeros_like(picked))
    spread = jnp.broadcast_to(shifted[:, None, :], (capacity, tile_width, padded_width))
    spread = spread.reshape(capacity, tile_width * padded_width)[
        :, : tile_width * (padded_width - 1)
    ]
    spread = spread.reshape(capacity, tile_width, padded_width - 1)[:, :, :kernel_width]
    lag_index = (
        jnp.arange(kernel_width, dtype=jnp.int32)[None, None, :]
        - jnp.arange(tile_width, dtype=jnp.int32)[None, :, None]
        - slot_move[:, None, None]
    )
    window = ((lag_index >= 0) & (lag_index < length)).astype(jnp.bfloat16)
    squares = slot_rows.astype(jnp.float32)
    squares = squares * squares
    square_high = squares.astype(jnp.bfloat16)
    square_low = (squares - square_high.astype(jnp.float32)).astype(jnp.bfloat16)
    tile_rows = tile_count + block_count - 1
    row_tiles = slot_rows.reshape(capacity, tile_rows, tile_width)
    high_tiles = square_high.reshape(capacity, tile_rows, tile_width)
    low_tiles = square_low.reshape(capacity, tile_rows, tile_width)
    numer = jnp.zeros((capacity, tile_count, tile_width), jnp.float32)
    energy = jnp.zeros((capacity, tile_count, tile_width), jnp.float32)
    for block in range(block_count):
        lo_col = block * tile_width
        kernel_part = spread[:, :, lo_col : lo_col + tile_width]
        window_part = window[:, :, lo_col : lo_col + tile_width]
        numer = numer + jnp.einsum(
            "gtk,gik->gti",
            row_tiles[:, block : block + tile_count],
            kernel_part,
            preferred_element_type=jnp.float32,
        )
        energy = energy + jnp.einsum(
            "gtk,gik->gti",
            high_tiles[:, block : block + tile_count],
            window_part,
            preferred_element_type=jnp.float32,
        )
        energy = energy + jnp.einsum(
            "gtk,gik->gti",
            low_tiles[:, block : block + tile_count],
            window_part,
            preferred_element_type=jnp.float32,
        )
    corr = numer * lax.rsqrt(energy / length + eps_value) / math.sqrt(length)
    contrib = corr.reshape(capacity, piece_len)
    partial_sum = jnp.dot(owner_table, contrib, precision=lax.Precision.HIGH)
    totals = lax.psum(partial_sum, "chan")
    stack = lax.dynamic_slice_in_dim(totals, group_index * TPL_DEV, TPL_DEV, 0)
    peaks = lax.pmax(jnp.max(jnp.abs(stack), axis=1), "tm")
    return (stack, peaks)


def solution(mesh):
    return jax.shard_map(
        on_device,
        mesh=mesh,
        in_specs=(P("chan", "tm"), P("chan", None, None), P(), P()),
        out_specs=(P("chan", "tm"), P("chan")),
        check_vma=False,
    )
```

profile of v0, /device:TPU:1, one launch (start us, length us, event | category | flops | bytes accessed | tf_op | source)
XLA Modules:
  0.0 827.7 jit_solution(4556879338427611375)
XLA Ops:
  7.2 1.5 copy.9
  9.7 1.3 collective-permute-start
  15.2 5.8 fusion
  22.8 2.7 fusion.17
  33.8 2.2 fusion.52
  36.0 42.5 %all-gather.2.cloned.1.call-done = f32[32,30,300]{2,1,0:T(8,128)} async-done(((f32[1,30,300]{2,1,0:T(8,128)}), f32[32,30,300]{2,1,0:T(8,128)}) %all-gather.2.cloned.1.call-update) | async-done | bytes 1152016 | tf_op jit(solution)/shard_map/all_gather | solution.py:41
  78.5 1.6 reduce_sum.40
  80.1 1.8 multiply_reduce_fusion
  81.9 1.8 multiply_convert_fusion
  84.8 389.9 %gather_fusion.2 = bf16[46080]{0:T(1024)(128)(2,1)S(1)} fusion(bf16[60,300]{1,0:T(8,128)(2,1)S(1)} %select_multiply_fusion, s32[46080]{0:T(1024)S(1)} %reshape.295), kind=kCustom, calls=%fused_computation.4 | custom fusion | bytes 552960 | tf_op jit(solution)/shard_map/jit(take_along_axis)/gather | solution.py:70
  475.0 5.2 broadcast_in_dim.63
  480.2 6.4 pad.10
  486.6 38.2 %copy.10 = bf16[8,8,128,768]{3,1,2,0:T(8,128)(2,1)S(1)} copy(bf16[8,8,128,768]{3,2,1,0:T(8,128)(2,1)S(1)} %bitcast.18) | data formatting | bytes 25165824
  524.8 5.2 slice.139
  530.0 28.4 %reshape.261 = bf16[60,128,767]{2,1,0:T(8,128)(2,1)} reshape(bf16[60,98176]{1,0:T(8,128)(2,1)} %slice.139) | data formatting | bytes 23562240 | tf_op jit(solution)/shard_map/reshape | solution.py:76
  558.4 2.7 fusion.21
  561.1 2.7 fusion.23
  563.8 2.7 fusion.25
  566.5 2.8 fusion.27
  569.2 2.7 fusion.82
  572.0 2.6 fusion.70
  576.4 221.7 %all-reduce.3.cloned.1.call-done = f32[32,4096]{1,0:T(8,128)} async-done(((f32[32,4096]{1,0:T(8,128)}), f32[32,4096]{1,0:T(8,128)}) %all-reduce.3.cloned.1.call-update) | async-done | bytes 524304 | tf_op jit(solution)/shard_map/psum | solution.py:118
  798.1 2.1 abs_reduce_fusion
  800.2 20.7 %pmax.7 = f32[1]{0:T(128)} all-reduce(f32[1]{0:T(128)} %bitcast.4), channel_id=1, replica_groups=mesh['chan'=32,'tm'=8] {'tm'}, use_global_device_ids=true, to_apply=%region_8.10 | all-reduce | flops 1 | bytes 8 | tf_op jit(solution)/shard_map/pmax | solution.py:120
  (59 shorter events, 18.3 us)
Async XLA Ops:
  7.2 13.9 %copy-start.1 = (bf16[96,4096]{1,0:T(8,128)(2,1)S(1)}, bf16[96,4096]{1,0:T(8,128)(2,1)}, u32[]{:S(2)}) copy-start(bf16[96,4096]{1,0:T(8,128)(2,1)} %param.6) | copy-start | bytes 2359300
  7.2 71.3 %all-gather.2.cloned.1.call-start = ((), (), s32[]{:S(2)}) async-start(), calls=%async_computation | async-start | bytes 1622016 | tf_op jit(solution)/shard_map/all_gather | solution.py:41
  8.7 789.3 %all-reduce.3.cloned.1.call-start = ((), (), s32[]{:S(2)}) async-start(), calls=%async_computation.1 | async-start | bytes 1048576 | tf_op jit(solution)/shard_map/psum | solution.py:118
  9.7 11.4 %collective-permute-start = (bf16[96,512]{1,0:T(8,128)(2,1)S(1)}, bf16[96,512]{1,0:T(8,128)(2,1)S(1)}, u32[]{:S(2)}, u32[]{:S(2)}) collective-permute-start(bf16[96,512]{1,0:T(8,128)(2,1)S(1)} %slice.100), channel_id=1, source_target_pairs={{1,0},{2,1},{3,2},{4,3},{5,4},{6,5},{7,6},{9,8},{10,9},{11,10},{12... | collective-permute-start | bytes 294920 | tf_op jit(solution)/shard_map/ppermute | solution.py:21
  22.4 3.2 copy-start
  566.5 5.5 copy-start.2
Sparse Core Ops, SparseCore 0:
  9.9 68.5 all-gather.1
  576.5 221.5 all-reduce.2
where the time goes:
time: 830 us; the launch traced here: 828 us
  local copies, waits for them, and re-layouts  482 us (58%)
  waiting for transfers between devices  264 us (32%)
  matrix products  30.3 us (4%)
  blocking collectives  20.7 us (2%)
  other arithmetic  14.7 us (2%)
  between operations  14.3 us (2%)
    gather x3, local copies, waits for them, and re-layouts, on_device(): jnp.take_along_axis(slot_wave, jnp.clip(source, 0, length - 1), axis=1)  390 us
    psum x1, waiting for transfers between devices, on_device(): totals = lax.psum(partial_sum, 'chan')  222 us
    unnamed x11, local copies, waits for them, and re-layouts  46.8 us
    all_gather x1, waiting for transfers between devices, on_device(): every_wave = lax.all_gather(waveforms, 'chan', axis=0, tiled=True)  42.5 us
    reshape x1, local copies, waits for them, and re-layouts, on_device(): spread.reshape(capacity, tile_width, padded_width - 1)[:, :, :kernel_width]  28.4 us
    pmax x1, blocking collectives, on_device(): peaks = lax.pmax(jnp.max(jnp.abs(stack), axis=1), 'tm')  20.7 us
  transfers between devices with their start and end apart: 3, of which 2 were waited for; matrix products, arithmetic and copies ran while one was open for 3% of the time, Pallas kernels for 0%

commit v1 on v0

v1 whole, which is shorter than its diff:
```python
import functools
import math

import jax
import jax.numpy as jnp
from jax import lax
from jax.experimental import pallas as pl
from jax.experimental.pallas import tpu as pltpu
from jax.sharding import PartitionSpec as P

LANES = 128
STATIONS = 20
PER = 3
SLOTS = STATIONS * PER
SEL = 64
HALO = 4
BLOCKS = 4
WAVE_BLOCKS = 3
HALVES = 2
EPS = 1e-05
MESH = pl.DeviceIdType.MESH


def each(count, body):
    def step(i, carry):
        body(i)
        return carry

    lax.fori_loop(0, count, step, 0)


def kernel(
    n_chan, n_tm, length,
    tab, seis, waves,
    stack_out, peak_out,
    x_in, halo_in, rows, turned, lhs, scale, band,
    normed, part_in, part_all, chosen, chosen_in, chosen_all,
    running, outgoing, incoming, peak_mine, peak_in,
    sems, in_sem,
):
    me = lax.axis_index("chan")
    now = lax.axis_index("tm")
    tiles = stack_out.shape[0]
    channels = x_in.shape[0]
    pitch = rows.shape[1]
    flat_rows = rows.reshape(channels * pitch, LANES)
    f32, bf16 = jnp.float32, jnp.bfloat16

    def wait_for(ref, blocks, sem):
        span = ref.at[pl.ds(0, blocks)]
        pltpu.make_async_copy(span, span, sem).wait()

    def chan_peer(d):
        return lax.rem(me + d, n_chan)

    def tm_peer(d):
        return lax.rem(now + d, n_tm)

    barrier = pltpu.get_barrier_semaphore()

    def greet_chan(i):
        pl.semaphore_signal(barrier, inc=1, device_id=(chan_peer(i + 1), now), device_id_type=MESH)

    def greet_tm(i):
        pl.semaphore_signal(barrier, inc=1, device_id=(me, tm_peer(i + 1)), device_id_type=MESH)

    each(n_tm - 1, greet_tm)
    each(n_chan - 1, greet_chan)
    load = pltpu.make_async_copy(seis, x_in, in_sem)
    load.start()

    w = waves[0]
    centered = w - jnp.mean(w, axis=-1, keepdims=True)
    factor = lax.rsqrt(jnp.mean(centered * centered, axis=-1, keepdims=True) + EPS) / math.sqrt(length)
    normed[...] = jnp.zeros_like(normed)
    normed[0 : w.shape[0], 0:length] = (centered * factor).astype(bf16)

    lag = lax.broadcasted_iota(jnp.int32, band.shape, 0) - lax.broadcasted_iota(jnp.int32, band.shape, 1)
    band[...] = jnp.where((lag >= 0) & (lag < length), 1.0, 0.0).astype(bf16)

    load.wait()
    pl.semaphore_wait(barrier, n_chan - 1 + n_tm - 1)

    halo = pltpu.make_async_remote_copy(
        src_ref=x_in.at[:, pl.ds(0, HALO * LANES)], dst_ref=halo_in,
        send_sem=sems.at[0], recv_sem=sems.at[1],
        device_id=(me, jnp.maximum(now - 1, 0)), device_id_type=MESH,
    )

    @pl.when(now > 0)
    def _():
        halo.start()

    sends_part = now < WAVE_BLOCKS * HALVES
    half_of = lax.rem(now, HALVES)
    block_of = jnp.minimum(now // HALVES, WAVE_BLOCKS - 1)
    part = normed.at[pl.ds(half_of * 16, 16), pl.ds(block_of * LANES, LANES)]

    def part_copy(i):
        return pltpu.make_async_remote_copy(
            src_ref=part, dst_ref=part_in.at[me],
            send_sem=sems.at[2], recv_sem=sems.at[3],
            device_id=(chan_peer(i + 1), now), device_id_type=MESH,
        )

    @pl.when(sends_part)
    def _():
        each(n_chan - 1, lambda i: part_copy(i).start())

    def lay(ref, first):
        for i in range(ref.shape[1] // LANES):
            for c in range(0, channels, 16):
                flat_rows[pl.ds(c * pitch + first + i, 16, stride=pitch), :] = ref[
                    c : c + 16, i * LANES : (i + 1) * LANES
                ].astype(f32)

    lay(x_in, 0)

    @pl.when(now < n_tm - 1)
    def _():
        halo.wait_recv()

    @pl.when(now == n_tm - 1)
    def _():
        halo_in[...] = jnp.zeros_like(halo_in)

    lay(halo_in, tiles)

    def chosen_copy(i):
        return pltpu.make_async_remote_copy(
            src_ref=chosen, dst_ref=chosen_in.at[now],
            send_sem=sems.at[4], recv_sem=sems.at[5],
            device_id=(me, tm_peer(i + 1)), device_id_type=MESH,
        )

    @pl.when(sends_part)
    def _():
        wait_for(part_in, n_chan - 1, sems.at[3])
        part_all[pl.ds(me * 16, 16), :] = part[...].astype(f32)

        def widen(i):
            peer = chan_peer(i + 1)
            part_all[pl.ds(peer * 16, 16), :] = part_in[peer].astype(f32)

        each(n_chan - 1, widen)
        picks = []
        for k in range(SLOTS):
            row = tab[2 * STATIONS + k // PER] + k % PER
            at = tab[STATIONS + k // PER] * 16 + lax.rem(row, 16)
            picks.append(part_all[at].reshape(1, LANES))
        for k in range(SLOTS, SEL):
            picks.append(jnp.zeros((1, LANES), f32))
        chosen[...] = jnp.concatenate(picks, axis=0).astype(bf16)
        each(n_tm - 1, lambda i: chosen_copy(i).start())

    lane = lax.broadcasted_iota(jnp.int32, (tiles, LANES), 1)

    def prepare(station):
        pieces, squares = [], []
        for d in range(PER):
            move = tab[3 * STATIONS + station * PER + d]
            record = rows[tab[station] + d]
            turned[d] = pltpu.roll(record, lax.rem(LANES - move, LANES), 1)
            here = lane < LANES - move
            parts = [turned[d, pl.ds(b, tiles), :] for b in range(BLOCKS + 1)]
            shifted = [jnp.where(here, parts[b], parts[b + 1]) for b in range(BLOCKS)]
            pieces.append(jnp.concatenate([s.astype(bf16) for s in shifted], axis=1))
            squares.append(jnp.concatenate([(s * s).astype(bf16) for s in shifted], axis=1))
        lhs[station] = jnp.concatenate(pieces, axis=0)
        energy = jnp.dot(jnp.concatenate(squares, axis=0), band[...], preferred_element_type=f32)
        scale[station] = lax.rsqrt(energy / length + EPS) / math.sqrt(length)

    each(STATIONS, prepare)

    for p in range(WAVE_BLOCKS * HALVES):
        @pl.when(now == p)
        def _():
            chosen_all[pl.ds(p * SEL, SEL), :] = chosen[...].astype(f32)

    @pl.when(sends_part)
    def _():
        wait_for(chosen_in, WAVE_BLOCKS * HALVES - 1, sems.at[5])

    @pl.when(jnp.logical_not(sends_part))
    def _():
        wait_for(chosen_in, WAVE_BLOCKS * HALVES, sems.at[5])

    def widen_chosen(i):
        peer = tm_peer(i + 1)

        @pl.when(peer < WAVE_BLOCKS * HALVES)
        def _():
            chosen_all[pl.ds(peer * SEL, SEL), :] = chosen_in[peer].astype(f32)

    each(n_tm - 1, widen_chosen)

    running[0] = jnp.zeros((tiles, LANES), f32)

    def correlate(station, total):
        for d in range(PER):
            k = station * PER + d
            half = (tab[2 * STATIONS + station] + d) // 16
            wave = [chosen_all[(HALVES * b + half) * SEL + k].reshape(1, LANES) for b in range(WAVE_BLOCKS)]
            wave.append(jnp.zeros((1, LANES), f32))
            wide = jnp.broadcast_to(jnp.concatenate(wave, axis=1), (LANES, BLOCKS * LANES))
            toeplitz = pltpu.roll(wide, 0, 1, stride=1, stride_axis=0).astype(bf16)
            numer = lax.dot_general(
                lhs[station, d * tiles : (d + 1) * tiles, :], toeplitz,
                (((1,), (1,)), ((), ())), preferred_element_type=f32,
            )
            total = total + numer * scale[station, d * tiles : (d + 1) * tiles, :]
        running[station + 1] = total
        return total

    lax.fori_loop(0, STATIONS, correlate, jnp.zeros((tiles, LANES), f32))

    ends = 3 * STATIONS + SLOTS

    def summed(template):
        return running[tab[ends + template + 1]] - running[tab[ends + template]]

    def stack_copy(i):
        peer = chan_peer(i + 1)
        return pltpu.make_async_remote_copy(
            src_ref=outgoing.at[peer], dst_ref=incoming.at[me],
            send_sem=sems.at[6], recv_sem=sems.at[7],
            device_id=(peer, now), device_id_type=MESH,
        )

    def send_stack(i):
        peer = chan_peer(i + 1)
        outgoing[peer] = summed(peer).astype(bf16)
        stack_copy(i).start()

    each(n_chan - 1, send_stack)
    stack = summed(me)
    wait_for(incoming, n_chan - 1, sems.at[7])
    stack = lax.fori_loop(
        0, n_chan - 1, lambda i, s: s + incoming[chan_peer(i + 1)].astype(f32), stack
    )
    stack_out[...] = stack
    peak_mine[...] = jnp.broadcast_to(jnp.max(jnp.abs(stack), keepdims=True), peak_mine.shape)

    def peak_copy(i):
        return pltpu.make_async_remote_copy(
            src_ref=peak_mine, dst_ref=peak_in.at[now],
            send_sem=sems.at[8], recv_sem=sems.at[9],
            device_id=(me, tm_peer(i + 1)), device_id_type=MESH,
        )

    each(n_tm - 1, lambda i: peak_copy(i).start())
    wait_for(peak_in, n_tm - 1, sems.at[9])
    peak_out[...] = lax.fori_loop(
        0, n_tm - 1, lambda i, s: jnp.maximum(s, peak_in[tm_peer(i + 1)]), peak_mine[...]
    )

    @pl.when(now > 0)
    def _():
        halo.wait_send()

    @pl.when(sends_part)
    def _():
        wait_for(part_in, n_chan - 1, sems.at[2])
        wait_for(chosen_in, n_tm - 1, sems.at[4])

    wait_for(outgoing, n_chan - 1, sems.at[6])
    wait_for(peak_in, n_tm - 1, sems.at[8])


def tables(channel_list, moveouts, group, channels):
    per_template = channel_list.shape[1] // PER
    first = channel_list[:, ::PER].reshape(-1)
    count = first.shape[0]
    index = jnp.arange(count, dtype=jnp.int32)
    local = first // channels == group
    rank = jnp.sum((index[None, :] < index[:, None]) & local[None, :], axis=1, dtype=jnp.int32)
    hit = ((rank[None, :] == jnp.arange(STATIONS, dtype=jnp.int32)[:, None]) & local[None, :]).astype(jnp.int32)
    chan = jnp.sum(hit * (first - group * channels)[None, :], axis=1)
    template = jnp.sum(hit * (index // per_template)[None, :], axis=1)
    row = jnp.sum(hit * (index % per_template * PER)[None, :], axis=1)
    move = jnp.sum(hit[:, :, None] * moveouts.reshape(1, count, PER), axis=1).reshape(-1)
    edges = jnp.arange(channel_list.shape[0] + 1, dtype=jnp.int32) * per_template
    ends = jnp.sum((index[None, :] < edges[:, None]) & local[None, :], axis=1, dtype=jnp.int32)
    return jnp.concatenate([chan, template, row, move, ends])


def on_device(n_chan, n_tm, seismic, waveforms, channel_list, moveouts):
    channels, piece = seismic.shape
    length = waveforms.shape[2]
    tiles = piece // LANES
    pitch = tiles + 8
    f32, bf16 = jnp.float32, jnp.bfloat16
    tab = tables(channel_list, moveouts, lax.axis_index("chan"), channels)
    stack, peak = pl.pallas_call(
        functools.partial(kernel, n_chan, n_tm, length),
        out_shape=(
            jax.ShapeDtypeStruct((tiles, LANES), f32),
            jax.ShapeDtypeStruct((8, LANES), f32),
        ),
        in_specs=[
            pl.BlockSpec(memory_space=pltpu.SMEM),
            pl.BlockSpec(memory_space=pl.ANY),
            pl.BlockSpec(memory_space=pltpu.VMEM),
        ],
        out_specs=[pl.BlockSpec(memory_space=pltpu.VMEM)] * 2,
        scratch_shapes=[
            pltpu.VMEM((channels, piece), bf16),
            pltpu.VMEM((channels, HALO * LANES), bf16),
            pltpu.VMEM((channels, pitch, LANES), f32),
            pltpu.VMEM((PER, pitch, LANES), f32),
            pltpu.VMEM((STATIONS, PER * tiles, BLOCKS * LANES), bf16),
            pltpu.VMEM((STATIONS, PER * tiles, LANES), f32),
            pltpu.VMEM((BLOCKS * LANES, LANES), bf16),
            pltpu.VMEM((32, WAVE_BLOCKS * LANES), bf16),
            pltpu.VMEM((n_chan, 16, LANES), bf16),
            pltpu.VMEM((n_chan * 16, LANES), f32),
            pltpu.VMEM((SEL, LANES), bf16),
            pltpu.VMEM((n_tm, SEL, LANES), bf16),
            pltpu.VMEM((WAVE_BLOCKS * HALVES * SEL, LANES), f32),
            pltpu.VMEM((STATIONS + 1, tiles, LANES), f32),
            pltpu.VMEM((n_chan, tiles, LANES), bf16),
            pltpu.VMEM((n_chan, tiles, LANES), bf16),
            pltpu.VMEM((8, LANES), f32),
            pltpu.VMEM((n_tm, 8, LANES), f32),
            pltpu.SemaphoreType.DMA((10,)),
            pltpu.SemaphoreType.DMA,
        ],
        compiler_params=pltpu.CompilerParams(
            collective_id=0, has_side_effects=True, vmem_limit_bytes=48 * 1024 * 1024
        ),
    )(tab, seismic, waveforms)
    return stack.reshape(1, piece), peak[0, 0:1]


def solution(mesh):
    return jax.shard_map(
        functools.partial(on_device, mesh.shape["chan"], mesh.shape["tm"]),
        mesh=mesh,
        in_specs=(P("chan", "tm"), P("chan", None, None), P(), P()),
        out_specs=(P("chan", "tm"), P("chan")),
        check_vma=False,
    )
```

time: 830 us -> 49.4 us (0.06)
  local copies, waits for them, and re-layouts: 482 us -> 4.47 us
  waiting for transfers between devices: 264 us -> 0 us
  Pallas kernels: 0 us -> 43.1 us
  matrix products: 30.3 us -> 0 us
  blocking collectives: 20.7 us -> 0 us
  other arithmetic: 14.7 us -> 0.72 us
  between operations: 14.3 us -> 0.73 us
    gather x8 -> x0, local copies, waits for them, and re-layouts: 393 us -> none  [the longest x3 390 us: on_device(): jnp.take_along_axis(slot_wave, jnp.clip(source, 0, length - 1), axis=1)]
    psum x1 -> x0, waiting for transfers between devices: 222 us -> none  [on_device(): totals = lax.psum(partial_sum, 'chan')]
    unnamed x11 -> x8, local copies, waits for them, and re-layouts: 46.8 us -> 2.36 us
    pallas_call x0 -> x1, Pallas kernels: none -> 43.1 us  [on_device(): pl.pallas_call(functools.partial(kernel, n_chan, n_tm, length), out_shape...]
    all_gather x1 -> x0, waiting for transfers between devices: 42.5 us -> none  [on_device(): every_wave = lax.all_gather(waveforms, 'chan', axis=0, tiled=True)]
    dot_general x16 -> x0, matrix products: 30.3 us -> none  [the longest x5 13.5 us: on_device(): jnp.einsum('gtk,gik->gti', row_tiles[:, block:block + tile_count], kernel...]
    reshape x4 -> x1, local copies, waits for them, and re-layouts: 30.4 us -> 0.1 us  [tables(): jnp.sum(hit[:, :, None] * moveouts.reshape(1, count, PER), axis=1)]
    pmax x1 -> x0, blocking collectives: 20.7 us -> none  [on_device(): peaks = lax.pmax(jnp.max(jnp.abs(stack), axis=1), 'tm')]
  transfers between devices with their start and end apart: 3 -> 0, of which waited for: 2 -> 0; matrix products, arithmetic and copies ran while one was open for 3% -> 0% of each run, Pallas kernels for 0% -> 0%
where the time goes in v1:
time: 49.4 us; the launch traced here: 49.1 us
  Pallas kernels  43.1 us (87%)
  local copies, waits for them, and re-layouts  4.47 us (9%)
  between operations  0.73 us (1%)
  other arithmetic  0.72 us (1%)
    pallas_call x1, Pallas kernels, on_device(): pl.pallas_call(functools.partial(kernel, n_chan, n_tm, length), out_shape...  43.1 us
    unnamed x8, local copies, waits for them, and re-layouts  2.36 us

profile of v1, /device:TPU:1, one launch (start us, length us, event | category | flops | bytes accessed | tf_op | source)
XLA Modules:
  0.0 49.1 jit_solution(11562523485046524454)
XLA Ops:
  0.6 0.8 %slice.6 = s32[32,10]{1,0:T(8,128)S(1)} slice(s32[32,30]{1,0:T(8,128)} %param.6), slice={[0:32:1], [0:30:3]} | slice | bytes 2560 | tf_op jit(solution)/shard_map/slice | solution.py:272
  1.5 0.1 and.56
  1.6 0.1 div.22
  1.8 0.1 convert_reduce_fusion
  1.9 0.0 copy-start.2
  1.9 0.1 sub.26
  2.0 0.2 select_reduce_fusion
  2.2 0.5 copy-done.2
  2.6 0.1 mul.72
  2.7 0.1 copy.8
  2.9 0.0 copy-start.1
  2.9 0.1 multiply_reduce_fusion
  3.0 0.1 copy.9
  3.1 0.1 reshape.104
  3.2 0.2 convert_reduce_fusion.1
  3.4 0.1 concatenate.3.tab
  3.5 0.2 copy-done.1
  3.7 0.0 copy-start
  3.7 1.1 %copy-done = bf16[96,4096]{1,0:T(8,128)(2,1)S(1)} copy-done((bf16[96,4096]{1,0:T(8,128)(2,1)S(1)}, bf16[96,4096]{1,0:T(8,128)(2,1)}, u32[]{:S(2)}) %copy-start) | copy-done | bytes 786456
  4.8 43.1 %shard_map.59 = (f32[32,128]{1,0:T(8,128)S(1)}, f32[8,128]{1,0:T(8,128)S(1)}) custom-call(s32[153]{0:T(256)S(1)} %concatenate.3.tab, bf16[96,4096]{1,0:T(8,128)(2,1)S(1)} %copy-done, f32[1,30,300]{2,1,0:T(8,128)S(1)} %copy.10.waves), custom_call_target="tpu_custom_call" | custom-call | tf_op jit(solution)/shard_map/pallas_call | solution.py:294
  47.9 0.5 %slice.7 = f32[1,1]{1,0:T(1,128)} slice(f32[8,128]{1,0:T(8,128)S(1)} %get-tuple-element.5), slice={[0:1], [0:1]} | slice | bytes 8 | tf_op jit(solution)/shard_map/slice | solution.py:332
  48.5 0.6 %copy.12 = f32[1,4096]{1,0:T(1,128)} copy(f32[1,4096]{1,0:T(1,128)S(1)} %bitcast.2) | data formatting | bytes 32768
  (7 shorter events, 0.1 us)
Async XLA Ops:
  1.9 0.7 %copy-start.2 = (s32[32,30]{1,0:T(8,128)S(1)}, s32[32,30]{1,0:T(8,128)}, u32[]{:S(2)}) copy-start(s32[32,30]{1,0:T(8,128)} %param.7) | copy-start | bytes 11524
  2.9 0.8 %copy-start.1 = (f32[1,30,300]{2,0,1:T(1,128)S(1)}, f32[1,30,300]{2,0,1:T(1,128)}, u32[]{:S(2)}) copy-start(f32[1,30,300]{2,0,1:T(1,128)} %param.5) | copy-start | bytes 108004
  3.7 1.1 %copy-start = (bf16[96,4096]{1,0:T(8,128)(2,1)S(1)}, bf16[96,4096]{1,0:T(8,128)(2,1)}, u32[]{:S(2)}) copy-start(bf16[96,4096]{1,0:T(8,128)(2,1)} %seis.1) | copy-start | bytes 2359300

commit v2 on v1

v2 whole, which is shorter than its diff:
```python
import functools
import math

import jax
import jax.numpy as jnp
from jax import lax
from jax.experimental import pallas as pl
from jax.experimental.pallas import tpu as pltpu
from jax.sharding import PartitionSpec as P

LANES = 128
STATIONS = 20
PER = 3
SLOTS = STATIONS * PER
SEL = 64
HALO = 4
BLOCKS = 4
WAVE_BLOCKS = 3
HALVES = 2
PARTS = WAVE_BLOCKS * HALVES
ROW = 4
EPS = 1e-05
MESH = pl.DeviceIdType.MESH


def each(count, body, unroll=1):
    def step(i, carry):
        for u in range(unroll):
            body(i * unroll + u)
        return carry

    assert count % unroll == 0
    lax.fori_loop(0, count // unroll, step, 0)


def before(x, axis):
    index = lax.broadcasted_iota(jnp.int32, x.shape, axis)
    step, total = 1, x
    while step < 32:
        total = total + jnp.where(index >= step, pltpu.roll(total, step, axis), 0)
        step *= 2
    return total - x


def kernel(
    n_chan, n_tm, length, channels,
    listed, moves, seis, waves,
    stack_out, peak_out,
    listed_in, moves_in, waves_in, x_in, halo_in, tab_v, tab,
    rows, turned, lhs, scale, band,
    normed, part_in, part_all, chosen, chosen_in, chosen_all,
    running, outgoing, incoming, peak_mine, peak_in,
    sems, in_sems,
):
    me = lax.axis_index("chan")
    now = lax.axis_index("tm")
    core = lax.rem(me, HALVES)
    across = lax.rem(now, ROW)
    row_start = now - across
    sibling = me + 1 - 2 * core
    tiles = stack_out.shape[0]
    pitch = rows.shape[1]
    flat_rows = rows.reshape(channels * pitch, LANES)
    half_tiles = tiles // 2
    f32, bf16, i32 = jnp.float32, jnp.bfloat16, jnp.int32

    def wait_for(ref, blocks, sem):
        span = ref.at[pl.ds(0, blocks)]
        pltpu.make_async_copy(span, span, sem).wait()

    def chan_peer(d):
        return lax.rem(me + d, n_chan)

    def tm_peer(d):
        return lax.rem(now + d, n_tm)

    def row_peer(d):
        return row_start + lax.rem(across + d, ROW)

    barrier = pltpu.get_barrier_semaphore()

    def greet(group, piece):
        pl.semaphore_signal(barrier, inc=1, device_id=(group, piece), device_id_type=MESH)

    each(n_chan - 1, lambda i: greet(chan_peer(i + 1), now))
    each(n_tm - 1, lambda i: greet(me, tm_peer(i + 1)))
    each(ROW - 1, lambda i: greet(sibling, row_peer(i + 1)))

    loads = [
        pltpu.make_async_copy(src, dst, in_sems.at[i])
        for i, (src, dst) in enumerate(
            ((waves, waves_in), (listed, listed_in), (moves, moves_in), (seis, x_in))
        )
    ]
    for copy in loads:
        copy.start()

    lag = lax.broadcasted_iota(i32, band.shape, 0) - lax.broadcasted_iota(i32, band.shape, 1)
    band[...] = jnp.where((lag >= 0) & (lag < length), 1.0, 0.0).astype(bf16)

    loads[0].wait()
    w = waves_in[0]
    centered = w - jnp.mean(w, axis=-1, keepdims=True)
    factor = lax.rsqrt(jnp.mean(centered * centered, axis=-1, keepdims=True) + EPS) / math.sqrt(length)
    normed[...] = jnp.zeros_like(normed)
    normed[0 : w.shape[0], 0:length] = (centered * factor).astype(bf16)

    pl.semaphore_wait(barrier, n_chan - 1 + n_tm - 1 + ROW - 1)

    halo = pltpu.make_async_remote_copy(
        src_ref=seis.at[:, pl.ds(0, HALO * LANES)], dst_ref=halo_in,
        send_sem=sems.at[0], recv_sem=sems.at[1],
        device_id=(me, jnp.maximum(now - 1, 0)), device_id_type=MESH,
    )

    sends_part = across < WAVE_BLOCKS
    block_of = jnp.minimum(across, WAVE_BLOCKS - 1)

    def part(half):
        return normed.at[pl.ds(half * 16, 16), pl.ds(block_of * LANES, LANES)]

    def part_copy(i):
        peer = chan_peer(i + 1)
        return pltpu.make_async_remote_copy(
            src_ref=part(lax.rem(peer, HALVES)), dst_ref=part_in.at[me],
            send_sem=sems.at[2], recv_sem=sems.at[3],
            device_id=(peer, now), device_id_type=MESH,
        )

    @pl.when(sends_part)
    def _():
        each(n_chan - 1, lambda i: part_copy(i).start())

    @pl.when(now > 0)
    def _():
        halo.start()

    loads[1].wait()
    loads[2].wait()
    templates, per_template = listed_in.shape
    names = listed_in[...]
    column = lax.broadcasted_iota(i32, names.shape, 1)
    key = jnp.full(names.shape, -1, i32)
    code = (lax.broadcasted_iota(i32, names.shape, 0) * 32 + column) * LANES + moves_in[...]
    counts = jnp.zeros((templates, 1), i32)
    for place, group in ((0, me), (SEL, sibling)):
        from_first = names - group * channels
        inside = (from_first >= 0) & (from_first < channels)
        mine = jnp.where(inside, 1, 0)
        in_row = before(mine, 1)
        full_row = jnp.sum(mine, axis=1, keepdims=True)
        rank = in_row + before(jnp.broadcast_to(full_row, mine.shape), 0)
        key = jnp.where(inside & (rank < SLOTS), rank + place, key)
        code = jnp.where(inside, code + from_first * (1 << 17), code)
        if place == 0:
            counts = full_row
    lane32 = lax.broadcasted_iota(i32, (templates, LANES), 1)
    found = jnp.zeros((templates, LANES), i32)
    for c in range(per_template):
        found = found + jnp.where(
            lane32 == jnp.broadcast_to(key[:, c : c + 1], lane32.shape),
            jnp.broadcast_to(code[:, c : c + 1], lane32.shape), 0,
        )
    ahead = jnp.where(
        lax.broadcasted_iota(i32, lane32.shape, 0) < lane32, jnp.broadcast_to(counts, lane32.shape), 0
    )
    tab_v[0:1, :] = jnp.sum(found, axis=0, keepdims=True)
    tab_v[1:2, :] = jnp.minimum(jnp.sum(ahead, axis=0, keepdims=True), SLOTS)
    to_scalars = pltpu.make_async_copy(tab_v, tab, in_sems.at[4])
    to_scalars.start()

    def lay(ref, first):
        for i in range(ref.shape[1] // LANES):
            for c in range(0, channels, 16):
                flat_rows[pl.ds(c * pitch + first + i, 16, stride=pitch), :] = ref[
                    c : c + 16, i * LANES : (i + 1) * LANES
                ].astype(f32)

    loads[3].wait()
    lay(x_in, 0)
    to_scalars.wait()

    def template_of(code):
        return (code >> 12) & 31

    def row_of(code):
        return (code >> 7) & 31

    lane = lax.broadcasted_iota(i32, (half_tiles, LANES), 1)
    together = 4

    def prepare(group, half):
        squares = []
        first = half * half_tiles
        for u in range(together):
            station = group * together + u
            for d in range(PER):
                entry = tab[0, station * PER + d]
                move = entry & (LANES - 1)
                record = rows[entry >> 17][first : first + half_tiles + 8]
                at = u * PER + d
                turned[at] = pltpu.roll(record, lax.rem(LANES - move, LANES), 1)
                here = lane < LANES - move
                parts = [turned[at, b : b + half_tiles, :] for b in range(BLOCKS + 1)]
                shifted = [jnp.where(here, parts[b], parts[b + 1]) for b in range(BLOCKS)]
                lhs[station, d, first : first + half_tiles, :] = jnp.concatenate(
                    [s.astype(bf16) for s in shifted], axis=1
                )
                squares.append(jnp.concatenate([(s * s).astype(bf16) for s in shifted], axis=1))
        energy = jnp.dot(jnp.concatenate(squares, axis=0), band[...], preferred_element_type=f32)
        factor = lax.rsqrt(energy / length + EPS) / math.sqrt(length)
        for u in range(together):
            for d in range(PER):
                at = (u * PER + d) * half_tiles
                scale[group * together + u, d, first : first + half_tiles, :] = factor[at : at + half_tiles]

    each(STATIONS // together, lambda g: prepare(g, 0))

    def chosen_copy(other, d):
        return pltpu.make_async_remote_copy(
            src_ref=chosen.at[other], dst_ref=chosen_in.at[block_of * HALVES + core],
            send_sem=sems.at[4], recv_sem=sems.at[5],
            device_id=(sibling if other else me, row_peer(d)), device_id_type=MESH,
        )

    @pl.when(sends_part)
    def _():
        wait_for(part_in, n_chan - 1, sems.at[3])
        part_all[pl.ds(me * 16, 16), :] = part(core)[...].astype(f32)

        def widen(i):
            peer = chan_peer(i + 1)
            part_all[pl.ds(peer * 16, 16), :] = part_in[peer].astype(f32)

        for i in range(n_chan - 1):
            widen(i)
        for other in (1, 0):
            picks = []
            for k in range(SLOTS):
                entry = tab[0, other * SEL + k]
                at = template_of(entry) * 16 + (row_of(entry) & 15)
                picks.append(part_all[at].reshape(1, LANES))
            for k in range(SLOTS, SEL):
                picks.append(jnp.zeros((1, LANES), f32))
            chosen[other] = jnp.concatenate(picks, axis=0).astype(bf16)
            if other:
                chosen_copy(1, 0).start()
            for d in (2, 1, 3):
                chosen_copy(other, d).start()

    @pl.when(now < n_tm - 1)
    def _():
        halo.wait_recv()

    @pl.when(now == n_tm - 1)
    def _():
        halo_in[...] = jnp.zeros_like(halo_in)

    lay(halo_in, tiles)
    each(STATIONS // together, lambda g: prepare(g, 1))

    @pl.when(sends_part)
    def _():
        wait_for(chosen_in, PARTS - 1, sems.at[5])

    @pl.when(jnp.logical_not(sends_part))
    def _():
        wait_for(chosen_in, PARTS, sems.at[5])

    for p in range(PARTS):
        own = sends_part & (block_of * HALVES + core == p)

        @pl.when(own)
        def _():
            chosen_all[p * SEL : (p + 1) * SEL, :] = chosen[0].astype(f32)

        @pl.when(jnp.logical_not(own))
        def _():
            chosen_all[p * SEL : (p + 1) * SEL, :] = chosen_in[p].astype(f32)

    running[0] = jnp.zeros((tiles, LANES), f32)

    def correlate(group, total):
        for u in range(together):
            station = group * together + u
            for d in range(PER):
                k = station * PER + d
                half = row_of(tab[0, k]) >> 4
                wave = [chosen_all[(HALVES * b + half) * SEL + k].reshape(1, LANES) for b in range(WAVE_BLOCKS)]
                wave.append(jnp.zeros((1, LANES), f32))
                wide = jnp.broadcast_to(jnp.concatenate(wave, axis=1), (LANES, BLOCKS * LANES))
                toeplitz = pltpu.roll(wide, 0, 1, stride=1, stride_axis=0).astype(bf16)
                numer = lax.dot_general(
                    lhs[station, d], toeplitz, (((1,), (1,)), ((), ())), preferred_element_type=f32,
                )
                total = total + numer * scale[station, d]
            running[station + 1] = total
        return total

    lax.fori_loop(0, STATIONS // together, correlate, jnp.zeros((tiles, LANES), f32))

    def summed(template):
        return running[tab[1, template + 1] // PER] - running[tab[1, template] // PER]

    def stack_copy(i):
        peer = chan_peer(i + 1)
        return pltpu.make_async_remote_copy(
            src_ref=outgoing.at[peer], dst_ref=incoming.at[me],
            send_sem=sems.at[6], recv_sem=sems.at[7],
            device_id=(peer, now), device_id_type=MESH,
        )

    def send_stack(i):
        peer = chan_peer(i + 1)
        outgoing[peer] = summed(peer).astype(bf16)
        stack_copy(i).start()

    for i in range(n_chan - 1):
        send_stack(i)
    stack = summed(me)
    wait_for(incoming, n_chan - 1, sems.at[7])
    for i in range(n_chan - 1):
        stack = stack + incoming[chan_peer(i + 1)].astype(f32)
    stack_out[...] = stack
    peak_mine[...] = jnp.broadcast_to(jnp.max(jnp.abs(stack), keepdims=True), peak_mine.shape)

    def peak_copy(i):
        return pltpu.make_async_remote_copy(
            src_ref=peak_mine, dst_ref=peak_in.at[now],
            send_sem=sems.at[8], recv_sem=sems.at[9],
            device_id=(me, tm_peer(i + 1)), device_id_type=MESH,
        )

    for i in range(n_tm - 1):
        peak_copy(i).start()
    wait_for(peak_in, n_tm - 1, sems.at[9])
    peak = peak_mine[...]
    for i in range(n_tm - 1):
        peak = jnp.maximum(peak, peak_in[tm_peer(i + 1)])
    peak_out[...] = peak

    @pl.when(now > 0)
    def _():
        halo.wait_send()

    @pl.when(sends_part)
    def _():
        wait_for(part_in, n_chan - 1, sems.at[2])
        wait_for(chosen_in, 2 * ROW - 1, sems.at[4])

    wait_for(outgoing, n_chan - 1, sems.at[6])
    wait_for(peak_in, n_tm - 1, sems.at[8])


def on_device(n_chan, n_tm, seismic, waveforms, channel_list, moveouts):
    channels, piece = seismic.shape
    length = waveforms.shape[2]
    tiles = piece // LANES
    pitch = tiles + 8
    f32, bf16, i32 = jnp.float32, jnp.bfloat16, jnp.int32
    stack, peak = pl.pallas_call(
        functools.partial(kernel, n_chan, n_tm, length, channels),
        out_shape=(
            jax.ShapeDtypeStruct((tiles, LANES), f32),
            jax.ShapeDtypeStruct((8, LANES), f32),
        ),
        in_specs=[pl.BlockSpec(memory_space=pltpu.HBM)] * 4,
        out_specs=[pl.BlockSpec(memory_space=pltpu.VMEM)] * 2,
        scratch_shapes=[
            pltpu.VMEM(channel_list.shape, i32),
            pltpu.VMEM(moveouts.shape, i32),
            pltpu.VMEM(waveforms.shape, f32),
            pltpu.VMEM((channels, piece), bf16),
            pltpu.VMEM((channels, HALO * LANES), bf16),
            pltpu.VMEM((8, LANES), i32),
            pltpu.SMEM((8, LANES), i32),
            pltpu.VMEM((channels, pitch, LANES), f32),
            pltpu.VMEM((4 * PER, tiles // 2 + 8, LANES), f32),
            pltpu.VMEM((STATIONS, PER, tiles, BLOCKS * LANES), bf16),
            pltpu.VMEM((STATIONS, PER, tiles, LANES), f32),
            pltpu.VMEM((BLOCKS * LANES, LANES), bf16),
            pltpu.VMEM((32, WAVE_BLOCKS * LANES), bf16),
            pltpu.VMEM((n_chan, 16, LANES), bf16),
            pltpu.VMEM((n_chan * 16, LANES), f32),
            pltpu.VMEM((2, SEL, LANES), bf16),
            pltpu.VMEM((2 * ROW, SEL, LANES), bf16),
            pltpu.VMEM((PARTS * SEL, LANES), f32),
            pltpu.VMEM((STATIONS + 1, tiles, LANES), f32),
            pltpu.VMEM((n_chan, tiles, LANES), bf16),
            pltpu.VMEM((n_chan, tiles, LANES), bf16),
            pltpu.VMEM((8, LANES), f32),
            pltpu.VMEM((n_tm, 8, LANES), f32),
            pltpu.SemaphoreType.DMA((10,)),
            pltpu.SemaphoreType.DMA((5,)),
        ],
        compiler_params=pltpu.CompilerParams(
            collective_id=0, has_side_effects=True, vmem_limit_bytes=48 * 1024 * 1024
        ),
    )(channel_list, moveouts, seismic, waveforms)
    return stack.reshape(1, piece), peak[0, 0:1]


def solution(mesh):
    return jax.shard_map(
        functools.partial(on_device, mesh.shape["chan"], mesh.shape["tm"]),
        mesh=mesh,
        in_specs=(P("chan", "tm"), P("chan", None, None), P(), P()),
        out_specs=(P("chan", "tm"), P("chan")),
        check_vma=False,
    )
```

time: 49.4 us -> 41.6 us (0.84)
  Pallas kernels: 43.1 us -> 37.7 us
  local copies, waits for them, and re-layouts: 4.47 us -> 3.06 us
  other arithmetic: 0.72 us -> 0 us
    pallas_call x1, Pallas kernels: 43.1 us -> 37.7 us  [on_device(): pl.pallas_call(functools.partial(kernel, n_chan, n_tm, length, channels),...]
    slice x1 -> x0, local copies, waits for them, and re-layouts: 0.82 us -> none  [tables(): first = channel_list[:, ::PER].reshape(-1)]
    reduce_sum x4 -> x0, other arithmetic: 0.63 us -> none  [the longest x1 0.18 us: tables(): jnp.sum((index[None, :] < edges[:, None]) & local[None, :], axis=1, dtype...]
where the time goes in v2:
time: 41.6 us; the launch traced here: 41.4 us
  Pallas kernels  37.7 us (91%)
  local copies, waits for them, and re-layouts  3.06 us (7%)
  between operations  0.67 us (2%)
    pallas_call x1, Pallas kernels, on_device(): pl.pallas_call(functools.partial(kernel, n_chan, n_tm, length, channels),...  37.7 us
    unnamed x8, local copies, waits for them, and re-layouts  2.55 us

profile of v2, /device:TPU:1, one launch (start us, length us, event | category | flops | bytes accessed | tf_op | source)
XLA Modules:
  0.0 41.4 jit_solution(3716314440128134836)
XLA Ops:
  0.6 0.0 copy-start.2
  0.6 0.0 copy-start.1
  0.7 0.8 %copy.6.waves = f32[1,30,300]{2,1,0:T(8,128)S(1)} copy(f32[1,30,300]{2,0,1:T(1,128)} %param.5) | data formatting | bytes 72000 | tf_op args[1]
  1.5 0.0 copy-done.2
  1.5 0.0 copy-done.1
  1.5 0.0 copy-start
  1.5 1.1 %copy-done = bf16[96,4096]{1,0:T(8,128)(2,1)S(1)} copy-done((bf16[96,4096]{1,0:T(8,128)(2,1)S(1)}, bf16[96,4096]{1,0:T(8,128)(2,1)}, u32[]{:S(2)}) %copy-start) | copy-done | bytes 786456
  2.6 37.7 %shard_map.59 = (f32[32,128]{1,0:T(8,128)S(1)}, f32[8,128]{1,0:T(8,128)S(1)}) custom-call(s32[32,30]{1,0:T(8,128)S(1)} %copy-done.1, s32[32,30]{1,0:T(8,128)S(1)} %copy-done.2, bf16[96,4096]{1,0:T(8,128)(2,1)S(1)} %copy-done, f32[1,30,300]{2,1,0:T(8,128)S(1)} %copy.6.waves), custom_call_target="tpu_custom_call" | custom-call | tf_op jit(solution)/shard_map/pallas_call | solution.py:361
  40.3 0.5 %slice.3 = f32[1,1]{1,0:T(1,128)} slice(f32[8,128]{1,0:T(8,128)S(1)} %get-tuple-element.5), slice={[0:1], [0:1]} | slice | bytes 8 | tf_op jit(solution)/shard_map/slice | solution.py:400
  40.8 0.6 %copy.8 = f32[1,4096]{1,0:T(1,128)} copy(f32[1,4096]{1,0:T(1,128)S(1)} %bitcast.2) | data formatting | bytes 32768
Async XLA Ops:
  0.6 0.8 %copy-start.2 = (s32[32,30]{1,0:T(8,128)S(1)}, s32[32,30]{1,0:T(8,128)}, u32[]{:S(2)}) copy-start(s32[32,30]{1,0:T(8,128)} %moves.1) | copy-start | bytes 11524
  0.6 0.8 %copy-start.1 = (s32[32,30]{1,0:T(8,128)S(1)}, s32[32,30]{1,0:T(8,128)}, u32[]{:S(2)}) copy-start(s32[32,30]{1,0:T(8,128)} %listed.1) | copy-start | bytes 11524
  1.5 1.1 %copy-start = (bf16[96,4096]{1,0:T(8,128)(2,1)S(1)}, bf16[96,4096]{1,0:T(8,128)(2,1)}, u32[]{:S(2)}) copy-start(bf16[96,4096]{1,0:T(8,128)(2,1)} %seis.1) | copy-start | bytes 2359300

commit v3 on v2

--- a/solution.py
+++ b/solution.py
@@ -19,7 +19,9 @@
 HALVES = 2
 PARTS = WAVE_BLOCKS * HALVES
 ROW = 4
+RING = 8
 EPS = 1e-05
+GRANT = 55200 * 1024
 MESH = pl.DeviceIdType.MESH
 
 
@@ -31,6 +33,13 @@
 
     assert count % unroll == 0
     lax.fori_loop(0, count // unroll, step, 0)
+
+
+def ring_offsets(n_chan):
+    chips = n_chan // HALVES
+    depth = min(RING, chips)
+    offsets = [(dy, dz) for dy in range(chips // depth) for dz in range(depth)]
+    return sorted(offsets, key=lambda o: (-(o[0] + min(o[1], depth - o[1])), o))
 
 
 def before(x, axis):
@@ -49,7 +58,7 @@
     listed_in, moves_in, waves_in, x_in, halo_in, tab_v, tab,
     rows, turned, lhs, scale, band,
     normed, part_in, part_all, chosen, chosen_in, chosen_all,
-    running, outgoing, incoming, peak_mine, peak_in,
+    running, pair_out, pair_in, outgoing, incoming, peak_mine, peak_in,
     sems, in_sems,
 ):
     me = lax.axis_index("chan")
@@ -68,8 +77,20 @@
         span = ref.at[pl.ds(0, blocks)]
         pltpu.make_async_copy(span, span, sem).wait()
 
-    def chan_peer(d):
-        return lax.rem(me + d, n_chan)
+    chip = me // HALVES
+    depth = min(RING, n_chan // HALVES)
+    offsets = ring_offsets(n_chan)
+
+    def chip_at(offset):
+        dy, dz = offset
+        y, z = chip // depth, lax.rem(chip, depth)
+        return lax.rem(y + dy, n_chan // HALVES // depth) * depth + lax.rem(z + dz, depth)
+
+    chan_peers = [
+        chip_at(offset) * HALVES + lax.rem(core + dc, HALVES)
+        for offset in offsets for dc in range(HALVES) if offset != (0, 0) or dc
+    ]
+    far_chips = [chip_at(offset) for offset in offsets if offset != (0, 0)]
 
     def tm_peer(d):
         return lax.rem(now + d, n_tm)
@@ -82,9 +103,14 @@
     def greet(group, piece):
         pl.semaphore_signal(barrier, inc=1, device_id=(group, piece), device_id_type=MESH)
 
-    each(n_chan - 1, lambda i: greet(chan_peer(i + 1), now))
-    each(n_tm - 1, lambda i: greet(me, tm_peer(i + 1)))
-    each(ROW - 1, lambda i: greet(sibling, row_peer(i + 1)))
+    for peer in chan_peers[: n_chan // 2]:
+        greet(peer, now)
+    for i in range(n_tm - 1):
+        greet(me, tm_peer(i + 1))
+    for i in range(ROW - 1):
+        greet(sibling, row_peer(i + 1))
+    for peer in chan_peers[n_chan // 2 :]:
+        greet(peer, now)
 
     loads = [
         pltpu.make_async_copy(src, dst, in_sems.at[i])
@@ -99,7 +125,7 @@
     band[...] = jnp.where((lag >= 0) & (lag < length), 1.0, 0.0).astype(bf16)
 
     loads[0].wait()
-    w = waves_in[0]
+    w = waves_in[:, 0, :]
     centered = w - jnp.mean(w, axis=-1, keepdims=True)
     factor = lax.rsqrt(jnp.mean(centered * centered, axis=-1, keepdims=True) + EPS) / math.sqrt(length)
     normed[...] = jnp.zeros_like(normed)
@@ -119,8 +145,7 @@
     def part(half):
         return normed.at[pl.ds(half * 16, 16), pl.ds(block_of * LANES, LANES)]
 
-    def part_copy(i):
-        peer = chan_peer(i + 1)
+    def part_copy(peer):
         return pltpu.make_async_remote_copy(
             src_ref=part(lax.rem(peer, HALVES)), dst_ref=part_in.at[me],
             send_sem=sems.at[2], recv_sem=sems.at[3],
@@ -129,7 +154,8 @@
 
     @pl.when(sends_part)
     def _():
-        each(n_chan - 1, lambda i: part_copy(i).start())
+        for peer in chan_peers:
+            part_copy(peer).start()
 
     @pl.when(now > 0)
     def _():
@@ -228,12 +254,8 @@
         wait_for(part_in, n_chan - 1, sems.at[3])
         part_all[pl.ds(me * 16, 16), :] = part(core)[...].astype(f32)
 
-        def widen(i):
-            peer = chan_peer(i + 1)
+        for peer in chan_peers:
             part_all[pl.ds(peer * 16, 16), :] = part_in[peer].astype(f32)
-
-        for i in range(n_chan - 1):
-            widen(i)
         for other in (1, 0):
             picks = []
             for k in range(SLOTS):
@@ -280,9 +302,11 @@
 
     running[0] = jnp.zeros((tiles, LANES), f32)
 
+    at_once = 10
+
     def correlate(group, total):
-        for u in range(together):
-            station = group * together + u
+        for u in range(at_once):
+            station = group * at_once + u
             for d in range(PER):
                 k = station * PER + d
                 half = row_of(tab[0, k]) >> 4
@@ -297,32 +321,37 @@
             running[station + 1] = total
         return total
 
-    lax.fori_loop(0, STATIONS // together, correlate, jnp.zeros((tiles, LANES), f32))
+    lax.fori_loop(0, STATIONS // at_once, correlate, jnp.zeros((tiles, LANES), f32))
 
     def summed(template):
         return running[tab[1, template + 1] // PER] - running[tab[1, template] // PER]
 
-    def stack_copy(i):
-        peer = chan_peer(i + 1)
+    pair = pltpu.make_async_remote_copy(
+        src_ref=pair_out, dst_ref=pair_in, send_sem=sems.at[10], recv_sem=sems.at[11],
+        device_id=(sibling, now), device_id_type=MESH,
+    )
+    for i in range(n_chan // HALVES):
+        pair_out[i] = summed(i * HALVES + 1 - core)
+    pair.start()
+
+    def stack_copy(place):
         return pltpu.make_async_remote_copy(
-            src_ref=outgoing.at[peer], dst_ref=incoming.at[me],
+            src_ref=outgoing.at[place], dst_ref=incoming.at[chip],
             send_sem=sems.at[6], recv_sem=sems.at[7],
-            device_id=(peer, now), device_id_type=MESH,
-        )
-
-    def send_stack(i):
-        peer = chan_peer(i + 1)
-        outgoing[peer] = summed(peer).astype(bf16)
-        stack_copy(i).start()
-
-    for i in range(n_chan - 1):
-        send_stack(i)
-    stack = summed(me)
-    wait_for(incoming, n_chan - 1, sems.at[7])
-    for i in range(n_chan - 1):
-        stack = stack + incoming[chan_peer(i + 1)].astype(f32)
+            device_id=(place * HALVES + core, now), device_id_type=MESH,
+        )
+
+    pair.wait_recv()
+    for place in far_chips:
+        outgoing[place] = (summed(place * HALVES + core) + pair_in[place]).astype(bf16)
+        stack_copy(place).start()
+    stack = summed(me) + pair_in[chip]
+    if far_chips:
+        wait_for(incoming, len(far_chips), sems.at[7])
+    for place in far_chips:
+        stack = stack + incoming[place].astype(f32)
     stack_out[...] = stack
-    peak_mine[...] = jnp.broadcast_to(jnp.max(jnp.abs(stack), keepdims=True), peak_mine.shape)
+    peak_mine[...] = jnp.max(jnp.abs(stack).reshape(tiles // 8, 8, LANES), axis=0)
 
     def peak_copy(i):
         return pltpu.make_async_remote_copy(
@@ -348,7 +377,9 @@
         wait_for(part_in, n_chan - 1, sems.at[2])
         wait_for(chosen_in, 2 * ROW - 1, sems.at[4])
 
-    wait_for(outgoing, n_chan - 1, sems.at[6])
+    pair.wait_send()
+    if far_chips:
+        wait_for(outgoing, len(far_chips), sems.at[6])
     wait_for(peak_in, n_tm - 1, sems.at[8])
 
 
@@ -369,7 +400,7 @@
         scratch_shapes=[
             pltpu.VMEM(channel_list.shape, i32),
             pltpu.VMEM(moveouts.shape, i32),
-            pltpu.VMEM(waveforms.shape, f32),
+            pltpu.VMEM((waveforms.shape[1], 1, length), f32),
             pltpu.VMEM((channels, piece), bf16),
             pltpu.VMEM((channels, HALO * LANES), bf16),
             pltpu.VMEM((8, LANES), i32),
@@ -386,18 +417,20 @@
             pltpu.VMEM((2 * ROW, SEL, LANES), bf16),
             pltpu.VMEM((PARTS * SEL, LANES), f32),
             pltpu.VMEM((STATIONS + 1, tiles, LANES), f32),
-            pltpu.VMEM((n_chan, tiles, LANES), bf16),
-            pltpu.VMEM((n_chan, tiles, LANES), bf16),
+            pltpu.VMEM((n_chan // HALVES, tiles, LANES), f32),
+            pltpu.VMEM((n_chan // HALVES, tiles, LANES), f32),
+            pltpu.VMEM((n_chan // HALVES, tiles, LANES), bf16),
+            pltpu.VMEM((n_chan // HALVES, tiles, LANES), bf16),
             pltpu.VMEM((8, LANES), f32),
             pltpu.VMEM((n_tm, 8, LANES), f32),
-            pltpu.SemaphoreType.DMA((10,)),
+            pltpu.SemaphoreType.DMA((12,)),
             pltpu.SemaphoreType.DMA((5,)),
         ],
         compiler_params=pltpu.CompilerParams(
-            collective_id=0, has_side_effects=True, vmem_limit_bytes=48 * 1024 * 1024
+            collective_id=0, has_side_effects=True, vmem_limit_bytes=GRANT
         ),
-    )(channel_list, moveouts, seismic, waveforms)
-    return stack.reshape(1, piece), peak[0, 0:1]
+    )(channel_list, moveouts, seismic, jnp.transpose(waveforms, (1, 0, 2)))
+    return stack.reshape(1, piece), jnp.max(peak).reshape(1)
 
 
 def solution(mesh):

time: 41.6 us -> 37.1 us (0.89)
  Pallas kernels: 37.7 us -> 35.2 us
  local copies, waits for them, and re-layouts: 3.06 us -> 0.6 us
  other arithmetic: 0 us -> 0.6 us
    pallas_call x1, Pallas kernels: 37.7 us -> 35.2 us  [on_device(): pl.pallas_call(functools.partial(kernel, n_chan, n_tm, length, channels),...]
    unnamed x8 -> x1, local copies, waits for them, and re-layouts: 2.55 us -> 0.6 us
    reduce_max x0 -> x1, other arithmetic: none -> 0.6 us  [on_device(): return (stack.reshape(1, piece), jnp.max(peak).reshape(1))]
    slice x1 -> x0, local copies, waits for them, and re-layouts: 0.51 us -> none  [on_device(): return (stack.reshape(1, piece), peak[0, 0:1])]
where the time goes in v3:
time: 37.1 us; the launch traced here: 37 us
  Pallas kernels  35.2 us (95%)
  between operations  0.64 us (2%)
  other arithmetic  0.6 us (2%)
  local copies, waits for them, and re-layouts  0.6 us (2%)
    pallas_call x1, Pallas kernels, on_device(): pl.pallas_call(functools.partial(kernel, n_chan, n_tm, length, channels),...  35.2 us

profile of v3, /device:TPU:1, one launch (start us, length us, event | category | flops | bytes accessed | tf_op | source)
XLA Modules:
  0.0 37.0 jit_solution(834407280543856615)
XLA Ops:
  0.6 35.2 %shard_map.59 = (f32[32,128]{1,0:T(8,128)S(1)}, f32[8,128]{1,0:T(8,128)S(1)}) custom-call(s32[32,30]{1,0:T(8,128)} %listed.1, s32[32,30]{1,0:T(8,128)} %moves.1, bf16[96,4096]{1,0:T(8,128)(2,1)} %seis.1, f32[30,1,300]{2,1,0:T(1,128)} %bitcast.4), custom_call_target="tpu_custom_call" | custom-call | tf_op jit(solution)/shard_map/pallas_call | solution.py:392
  35.8 0.6 %reduce_max.9 = f32[]{:T(128)} reduce(f32[8,128]{1,0:T(8,128)S(1)} %get-tuple-element.5, f32[]{:T(128)} %constant.0.clone.1), dimensions={0,1}, to_apply=%region_0.0 | reduce | flops 1023 | bytes 4104 | tf_op jit(solution)/shard_map/reduce_max | solution.py:433
  36.4 0.6 %copy.7 = f32[1,4096]{1,0:T(1,128)} copy(f32[1,4096]{1,0:T(1,128)S(1)} %bitcast.3) | data formatting | bytes 32768

commit v4 on v3

--- a/solution.py
+++ b/solution.py
@@ -9,6 +9,7 @@
 from jax.sharding import PartitionSpec as P
 
 LANES = 128
+HALF_LANES = 64
 STATIONS = 20
 PER = 3
 SLOTS = STATIONS * PER
@@ -213,6 +214,7 @@
         return (code >> 7) & 31
 
     lane = lax.broadcasted_iota(i32, (half_tiles, LANES), 1)
+    left = lane < HALF_LANES
     together = 4
 
     def prepare(group, half):
@@ -229,9 +231,13 @@
                 here = lane < LANES - move
                 parts = [turned[at, b : b + half_tiles, :] for b in range(BLOCKS + 1)]
                 shifted = [jnp.where(here, parts[b], parts[b + 1]) for b in range(BLOCKS)]
-                lhs[station, d, first : first + half_tiles, :] = jnp.concatenate(
-                    [s.astype(bf16) for s in shifted], axis=1
-                )
+                swung = [pltpu.roll(s, HALF_LANES, 1) for s in shifted]
+                later = [jnp.where(left, swung[b], swung[b + 1]) for b in range(WAVE_BLOCKS)]
+                for phase, tile in enumerate((shifted[:WAVE_BLOCKS], later)):
+                    at_row = (at % 2 * 2 + phase) * tiles + first
+                    lhs[group * (together * PER // 2) + at // 2, at_row : at_row + half_tiles, :] = jnp.concatenate(
+                        [s.astype(bf16) for s in tile], axis=1
+                    )
                 squares.append(jnp.concatenate([(s * s).astype(bf16) for s in shifted], axis=1))
         energy = jnp.dot(jnp.concatenate(squares, axis=0), band[...], preferred_element_type=f32)
         factor = lax.rsqrt(energy / length + EPS) / math.sqrt(length)
@@ -302,22 +308,31 @@
 
     running[0] = jnp.zeros((tiles, LANES), f32)
 
-    at_once = 10
+    at_once = 20
+    left_all = lax.broadcasted_iota(i32, (tiles, LANES), 1) < HALF_LANES
+
+    def toeplitz_of(k):
+        half = row_of(tab[0, k]) >> 4
+        wave = [chosen_all[(HALVES * b + half) * SEL + k].reshape(1, LANES) for b in range(WAVE_BLOCKS)]
+        wide = jnp.broadcast_to(jnp.concatenate(wave, axis=1), (HALF_LANES, WAVE_BLOCKS * LANES))
+        return pltpu.roll(wide, 0, 1, stride=1, stride_axis=0).astype(bf16)
 
     def correlate(group, total):
+        numers = []
+        for p in range(at_once * PER // 2):
+            pair = group * (at_once * PER // 2) + p
+            both = lax.dot_general(
+                lhs[pair], jnp.concatenate([toeplitz_of(pair * 2), toeplitz_of(pair * 2 + 1)], axis=0),
+                (((1,), (1,)), ((), ())), preferred_element_type=f32,
+            )
+            first, second, third, fourth = (both[i * tiles : (i + 1) * tiles] for i in range(4))
+            swapped = pltpu.roll(jnp.where(left_all, second, third), HALF_LANES, 1)
+            numers.append(jnp.where(left_all, first, swapped))
+            numers.append(jnp.where(left_all, swapped, fourth))
         for u in range(at_once):
             station = group * at_once + u
             for d in range(PER):
-                k = station * PER + d
-                half = row_of(tab[0, k]) >> 4
-                wave = [chosen_all[(HALVES * b + half) * SEL + k].reshape(1, LANES) for b in range(WAVE_BLOCKS)]
-                wave.append(jnp.zeros((1, LANES), f32))
-                wide = jnp.broadcast_to(jnp.concatenate(wave, axis=1), (LANES, BLOCKS * LANES))
-                toeplitz = pltpu.roll(wide, 0, 1, stride=1, stride_axis=0).astype(bf16)
-                numer = lax.dot_general(
-                    lhs[station, d], toeplitz, (((1,), (1,)), ((), ())), preferred_element_type=f32,
-                )
-                total = total + numer * scale[station, d]
+                total = total + numers[u * PER + d] * scale[station, d]
             running[station + 1] = total
         return total
 
@@ -407,7 +422,7 @@
             pltpu.SMEM((8, LANES), i32),
             pltpu.VMEM((channels, pitch, LANES), f32),
             pltpu.VMEM((4 * PER, tiles // 2 + 8, LANES), f32),
-            pltpu.VMEM((STATIONS, PER, tiles, BLOCKS * LANES), bf16),
+            pltpu.VMEM((SLOTS // 2, 4 * tiles, WAVE_BLOCKS * LANES), bf16),
             pltpu.VMEM((STATIONS, PER, tiles, LANES), f32),
             pltpu.VMEM((BLOCKS * LANES, LANES), bf16),
             pltpu.VMEM((32, WAVE_BLOCKS * LANES), bf16),

time: 37.1 us -> 35.4 us (0.954)
  Pallas kernels: 35.2 us -> 33.5 us
    pallas_call x1, Pallas kernels: 35.2 us -> 33.5 us  [on_device(): pl.pallas_call(functools.partial(kernel, n_chan, n_tm, length, channels),...]
where the time goes in v4:
time: 35.4 us; the launch traced here: 35.3 us
  Pallas kernels  33.5 us (95%)
  between operations  0.64 us (2%)
  other arithmetic  0.6 us (2%)
  local copies, waits for them, and re-layouts  0.6 us (2%)
    pallas_call x1, Pallas kernels, on_device(): pl.pallas_call(functools.partial(kernel, n_chan, n_tm, length, channels),...  33.5 us

profile of v4, /device:TPU:1, one launch (start us, length us, event | category | flops | bytes accessed | tf_op | source)
XLA Modules:
  0.0 35.3 jit_solution(7536541323167783233)
XLA Ops:
  0.6 33.5 %shard_map.59 = (f32[32,128]{1,0:T(8,128)S(1)}, f32[8,128]{1,0:T(8,128)S(1)}) custom-call(s32[32,30]{1,0:T(8,128)} %listed.1, s32[32,30]{1,0:T(8,128)} %moves.1, bf16[96,4096]{1,0:T(8,128)(2,1)} %seis.1, f32[30,1,300]{2,1,0:T(1,128)} %bitcast.4), custom_call_target="tpu_custom_call" | custom-call | tf_op jit(solution)/shard_map/pallas_call | solution.py:407
  34.1 0.6 %reduce_max.9 = f32[]{:T(128)} reduce(f32[8,128]{1,0:T(8,128)S(1)} %get-tuple-element.5, f32[]{:T(128)} %constant.0.clone.1), dimensions={0,1}, to_apply=%region_0.0 | reduce | flops 1023 | bytes 4104 | tf_op jit(solution)/shard_map/reduce_max | solution.py:448
  34.7 0.6 %copy.7 = f32[1,4096]{1,0:T(1,128)} copy(f32[1,4096]{1,0:T(1,128)S(1)} %bitcast.3) | data formatting | bytes 32768

commit v5 on v4

--- a/solution.py
+++ b/solution.py
@@ -21,6 +21,7 @@
 PARTS = WAVE_BLOCKS * HALVES
 ROW = 4
 RING = 8
+PAIR_PIECES = 2
 EPS = 1e-05
 GRANT = 55200 * 1024
 MESH = pl.DeviceIdType.MESH
@@ -58,9 +59,9 @@
     stack_out, peak_out,
     listed_in, moves_in, waves_in, x_in, halo_in, tab_v, tab,
     rows, turned, lhs, scale, band,
-    normed, part_in, part_all, chosen, chosen_in, chosen_all,
-    running, pair_out, pair_in, outgoing, incoming, peak_mine, peak_in,
-    sems, in_sems,
+    normed, part_in, takes, chosen, chosen_in, chosen_all,
+    running, mine_out, pair_out, pair_in, outgoing, incoming, peak_mine, peak_in,
+    sems, pair_sems, in_sems,
 ):
     me = lax.axis_index("chan")
     now = lax.axis_index("tm")
@@ -101,6 +102,14 @@
 
     barrier = pltpu.get_barrier_semaphore()
 
+    loads = [
+        pltpu.make_async_copy(src, dst, in_sems.at[i])
+        for i, (src, dst) in enumerate(
+            ((waves, waves_in), (listed, listed_in), (moves, moves_in), (seis, x_in))
+        )
+    ]
+    loads[0].start()
+
     def greet(group, piece):
         pl.semaphore_signal(barrier, inc=1, device_id=(group, piece), device_id_type=MESH)
 
@@ -113,17 +122,8 @@
     for peer in chan_peers[n_chan // 2 :]:
         greet(peer, now)
 
-    loads = [
-        pltpu.make_async_copy(src, dst, in_sems.at[i])
-        for i, (src, dst) in enumerate(
-            ((waves, waves_in), (listed, listed_in), (moves, moves_in), (seis, x_in))
-        )
-    ]
-    for copy in loads:
+    for copy in loads[1:]:
         copy.start()
-
-    lag = lax.broadcasted_iota(i32, band.shape, 0) - lax.broadcasted_iota(i32, band.shape, 1)
-    band[...] = jnp.where((lag >= 0) & (lag < length), 1.0, 0.0).astype(bf16)
 
     loads[0].wait()
     w = waves_in[:, 0, :]
@@ -157,10 +157,14 @@
     def _():
         for peer in chan_peers:
             part_copy(peer).start()
+        part_in[me] = part(core)[...]
 
     @pl.when(now > 0)
     def _():
         halo.start()
+
+    lag = lax.broadcasted_iota(i32, band.shape, 0) - lax.broadcasted_iota(i32, band.shape, 1)
+    band[...] = jnp.where((lag >= 0) & (lag < length), 1.0, 0.0).astype(bf16)
 
     loads[1].wait()
     loads[2].wait()
@@ -207,11 +211,13 @@
     lay(x_in, 0)
     to_scalars.wait()
 
-    def template_of(code):
-        return (code >> 12) & 31
-
-    def row_of(code):
-        return (code >> 7) & 31
+    entries = tab_v[0:1, :]
+    rows_of = (entries >> 7) & 31
+    taken = jnp.where(rows_of // 16 == core, ((entries >> 12) & 31) * 16 + rows_of % 16, -1)
+    taken = jnp.broadcast_to(taken, (n_chan * 16, LANES))
+    hot = jnp.where(lax.broadcasted_iota(i32, taken.shape, 0) == taken, 1.0, 0.0)
+    for b in range(n_chan * 16 // LANES):
+        takes[:, b * LANES : (b + 1) * LANES] = hot[b * LANES : (b + 1) * LANES].T.astype(bf16)
 
     lane = lax.broadcasted_iota(i32, (half_tiles, LANES), 1)
     left = lane < HALF_LANES
@@ -258,19 +264,11 @@
     @pl.when(sends_part)
     def _():
         wait_for(part_in, n_chan - 1, sems.at[3])
-        part_all[pl.ds(me * 16, 16), :] = part(core)[...].astype(f32)
-
-        for peer in chan_peers:
-            part_all[pl.ds(peer * 16, 16), :] = part_in[peer].astype(f32)
+        picked = jnp.dot(
+            takes[...], part_in[...].reshape(n_chan * 16, LANES), preferred_element_type=f32
+        ).astype(bf16)
         for other in (1, 0):
-            picks = []
-            for k in range(SLOTS):
-                entry = tab[0, other * SEL + k]
-                at = template_of(entry) * 16 + (row_of(entry) & 15)
-                picks.append(part_all[at].reshape(1, LANES))
-            for k in range(SLOTS, SEL):
-                picks.append(jnp.zeros((1, LANES), f32))
-            chosen[other] = jnp.concatenate(picks, axis=0).astype(bf16)
+            chosen[other] = picked[other * SEL : (other + 1) * SEL]
             if other:
                 chosen_copy(1, 0).start()
             for d in (2, 1, 3):
@@ -300,11 +298,11 @@
 
         @pl.when(own)
         def _():
-            chosen_all[p * SEL : (p + 1) * SEL, :] = chosen[0].astype(f32)
-
-        @pl.when(jnp.logical_not(own))
-        def _():
-            chosen_all[p * SEL : (p + 1) * SEL, :] = chosen_in[p].astype(f32)
+            chosen_in[p] = chosen[0]
+
+    for b in range(WAVE_BLOCKS):
+        halves = [chosen_in[b * HALVES + h].astype(f32) for h in range(HALVES)]
+        chosen_all[:, b * LANES : (b + 1) * LANES] = halves[0] + halves[1]
 
     running[0] = jnp.zeros((tiles, LANES), f32)
 
@@ -312,9 +310,7 @@
     left_all = lax.broadcasted_iota(i32, (tiles, LANES), 1) < HALF_LANES
 
     def toeplitz_of(k):
-        half = row_of(tab[0, k]) >> 4
-        wave = [chosen_all[(HALVES * b + half) * SEL + k].reshape(1, LANES) for b in range(WAVE_BLOCKS)]
-        wide = jnp.broadcast_to(jnp.concatenate(wave, axis=1), (HALF_LANES, WAVE_BLOCKS * LANES))
+        wide = jnp.broadcast_to(chosen_all[pl.ds(k, 1), :], (HALF_LANES, WAVE_BLOCKS * LANES))
         return pltpu.roll(wide, 0, 1, stride=1, stride_axis=0).astype(bf16)
 
     def correlate(group, total):
@@ -341,13 +337,21 @@
     def summed(template):
         return running[tab[1, template + 1] // PER] - running[tab[1, template] // PER]
 
-    pair = pltpu.make_async_remote_copy(
-        src_ref=pair_out, dst_ref=pair_in, send_sem=sems.at[10], recv_sem=sems.at[11],
-        device_id=(sibling, now), device_id_type=MESH,
-    )
-    for i in range(n_chan // HALVES):
-        pair_out[i] = summed(i * HALVES + 1 - core)
-    pair.start()
+    places = far_chips + [chip]
+    share = len(places) // PAIR_PIECES
+
+    def pair_copy(piece):
+        span = pl.ds(piece * share, share)
+        return pltpu.make_async_remote_copy(
+            src_ref=pair_out.at[span], dst_ref=pair_in.at[span],
+            send_sem=pair_sems.at[0, piece], recv_sem=pair_sems.at[1, piece],
+            device_id=(sibling, now), device_id_type=MESH,
+        )
+
+    for piece in range(PAIR_PIECES):
+        for i in range(piece * share, (piece + 1) * share):
+            pair_out[i] = summed(places[i] * HALVES + 1 - core)
+        pair_copy(piece).start()
 
     def stack_copy(place):
         return pltpu.make_async_remote_copy(
@@ -356,11 +360,16 @@
             device_id=(place * HALVES + core, now), device_id_type=MESH,
         )
 
-    pair.wait_recv()
-    for place in far_chips:
-        outgoing[place] = (summed(place * HALVES + core) + pair_in[place]).astype(bf16)
-        stack_copy(place).start()
-    stack = summed(me) + pair_in[chip]
+    for i, place in enumerate(places):
+        mine_out[i] = summed(place * HALVES + core)
+    stack = jnp.zeros((tiles, LANES), f32)
+    for i, place in enumerate(places):
+        if i % share == 0:
+            pair_copy(i // share).wait_recv()
+        stack = mine_out[i] + pair_in[i]
+        if i < len(far_chips):
+            outgoing[place] = stack.astype(bf16)
+            stack_copy(place).start()
     if far_chips:
         wait_for(incoming, len(far_chips), sems.at[7])
     for place in far_chips:
@@ -392,7 +401,8 @@
         wait_for(part_in, n_chan - 1, sems.at[2])
         wait_for(chosen_in, 2 * ROW - 1, sems.at[4])
 
-    pair.wait_send()
+    for piece in range(PAIR_PIECES):
+        pair_copy(piece).wait_send()
     if far_chips:
         wait_for(outgoing, len(far_chips), sems.at[6])
     wait_for(peak_in, n_tm - 1, sems.at[8])
@@ -427,18 +437,20 @@
             pltpu.VMEM((BLOCKS * LANES, LANES), bf16),
             pltpu.VMEM((32, WAVE_BLOCKS * LANES), bf16),
             pltpu.VMEM((n_chan, 16, LANES), bf16),
-            pltpu.VMEM((n_chan * 16, LANES), f32),
+            pltpu.VMEM((2 * SEL, n_chan * 16), bf16),
             pltpu.VMEM((2, SEL, LANES), bf16),
             pltpu.VMEM((2 * ROW, SEL, LANES), bf16),
-            pltpu.VMEM((PARTS * SEL, LANES), f32),
+            pltpu.VMEM((SEL, WAVE_BLOCKS * LANES), f32),
             pltpu.VMEM((STATIONS + 1, tiles, LANES), f32),
+            pltpu.VMEM((n_chan // HALVES, tiles, LANES), f32),
             pltpu.VMEM((n_chan // HALVES, tiles, LANES), f32),
             pltpu.VMEM((n_chan // HALVES, tiles, LANES), f32),
             pltpu.VMEM((n_chan // HALVES, tiles, LANES), bf16),
             pltpu.VMEM((n_chan // HALVES, tiles, LANES), bf16),
             pltpu.VMEM((8, LANES), f32),
             pltpu.VMEM((n_tm, 8, LANES), f32),
-            pltpu.SemaphoreType.DMA((12,)),
+            pltpu.SemaphoreType.DMA((10,)),
+            pltpu.SemaphoreType.DMA((2, PAIR_PIECES)),
             pltpu.SemaphoreType.DMA((5,)),
         ],
         compiler_params=pltpu.CompilerParams(

time: 35.4 us -> 35 us (0.989)
  Pallas kernels: 33.5 us -> 33 us
    pallas_call x1, Pallas kernels: 33.5 us -> 33 us  [on_device(): pl.pallas_call(functools.partial(kernel, n_chan, n_tm, length, channels),...]
where the time goes in v5:
time: 35 us; the launch traced here: 34.9 us
  Pallas kernels  33 us (94%)
  between operations  0.64 us (2%)
  other arithmetic  0.6 us (2%)
  local copies, waits for them, and re-layouts  0.6 us (2%)
    pallas_call x1, Pallas kernels, on_device(): pl.pallas_call(functools.partial(kernel, n_chan, n_tm, length, channels),...  33 us

profile of v5, /device:TPU:1, one launch (start us, length us, event | category | flops | bytes accessed | tf_op | source)
XLA Modules:
  0.0 34.9 jit_solution(14185686099262100876)
XLA Ops:
  0.6 33.0 %shard_map.59 = (f32[32,128]{1,0:T(8,128)S(1)}, f32[8,128]{1,0:T(8,128)S(1)}) custom-call(s32[32,30]{1,0:T(8,128)} %listed.1, s32[32,30]{1,0:T(8,128)} %moves.1, bf16[96,4096]{1,0:T(8,128)(2,1)} %seis.1, f32[30,1,300]{2,1,0:T(1,128)} %bitcast.4), custom_call_target="tpu_custom_call" | custom-call | tf_op jit(solution)/shard_map/pallas_call | solution.py:417
  33.7 0.6 %reduce_max.9 = f32[]{:T(128)} reduce(f32[8,128]{1,0:T(8,128)S(1)} %get-tuple-element.5, f32[]{:T(128)} %constant.0.clone.1), dimensions={0,1}, to_apply=%region_0.0 | reduce | flops 1023 | bytes 4104 | tf_op jit(solution)/shard_map/reduce_max | solution.py:460
  34.3 0.6 %copy.7 = f32[1,4096]{1,0:T(1,128)} copy(f32[1,4096]{1,0:T(1,128)S(1)} %bitcast.3) | data formatting | bytes 32768

commit v6 on v5

--- a/solution.py
+++ b/solution.py
@@ -269,10 +269,11 @@
         ).astype(bf16)
         for other in (1, 0):
             chosen[other] = picked[other * SEL : (other + 1) * SEL]
-            if other:
-                chosen_copy(1, 0).start()
-            for d in (2, 1, 3):
-                chosen_copy(other, d).start()
+        for d in (2, 1, 3, 0):
+            for other in (1, 0):
+                if other or d:
+                    chosen_copy(other, d).start()
+        chosen_in[block_of * HALVES + core] = chosen[0]
 
     @pl.when(now < n_tm - 1)
     def _():
@@ -292,13 +293,6 @@
     @pl.when(jnp.logical_not(sends_part))
     def _():
         wait_for(chosen_in, PARTS, sems.at[5])
-
-    for p in range(PARTS):
-        own = sends_part & (block_of * HALVES + core == p)
-
-        @pl.when(own)
-        def _():
-            chosen_in[p] = chosen[0]
 
     for b in range(WAVE_BLOCKS):
         halves = [chosen_in[b * HALVES + h].astype(f32) for h in range(HALVES)]

time: 35 us -> 34.9 us (level)
  no operation moved by 1% of the time
where the time goes in v6:
time: 34.9 us; the launch traced here: 34.8 us
  Pallas kernels  32.9 us (94%)
  between operations  0.64 us (2%)
  other arithmetic  0.6 us (2%)
  local copies, waits for them, and re-layouts  0.6 us (2%)
    pallas_call x1, Pallas kernels, on_device(): pl.pallas_call(functools.partial(kernel, n_chan, n_tm, length, channels),...  32.9 us

profile of v6, /device:TPU:1, one launch (start us, length us, event | category | flops | bytes accessed | tf_op | source)
XLA Modules:
  0.0 34.8 jit_solution(14199260147151986283)
XLA Ops:
  0.6 32.9 %shard_map.59 = (f32[32,128]{1,0:T(8,128)S(1)}, f32[8,128]{1,0:T(8,128)S(1)}) custom-call(s32[32,30]{1,0:T(8,128)} %listed.1, s32[32,30]{1,0:T(8,128)} %moves.1, bf16[96,4096]{1,0:T(8,128)(2,1)} %seis.1, f32[30,1,300]{2,1,0:T(1,128)} %bitcast.4), custom_call_target="tpu_custom_call" | custom-call | tf_op jit(solution)/shard_map/pallas_call | solution.py:411
  33.5 0.6 %reduce_max.9 = f32[]{:T(128)} reduce(f32[8,128]{1,0:T(8,128)S(1)} %get-tuple-element.5, f32[]{:T(128)} %constant.0.clone.1), dimensions={0,1}, to_apply=%region_0.0 | reduce | flops 1023 | bytes 4104 | tf_op jit(solution)/shard_map/reduce_max | solution.py:454
  34.1 0.6 %copy.7 = f32[1,4096]{1,0:T(1,128)} copy(f32[1,4096]{1,0:T(1,128)S(1)} %bitcast.3) | data formatting | bytes 32768

commit v7 on v6

--- a/solution.py
+++ b/solution.py
@@ -22,6 +22,7 @@
 ROW = 4
 RING = 8
 PAIR_PIECES = 2
+DIRECT = 1
 EPS = 1e-05
 GRANT = 55200 * 1024
 MESH = pl.DeviceIdType.MESH
@@ -331,11 +332,27 @@
     def summed(template):
         return running[tab[1, template + 1] // PER] - running[tab[1, template] // PER]
 
-    places = far_chips + [chip]
-    share = len(places) // PAIR_PIECES
+    def stack_copy(peer):
+        return pltpu.make_async_remote_copy(
+            src_ref=outgoing.at[peer], dst_ref=incoming.at[me],
+            send_sem=sems.at[6], recv_sem=sems.at[7],
+            device_id=(peer, now), device_id_type=MESH,
+        )
+
+    def send_stack(peer, total):
+        outgoing[peer] = total.astype(bf16)
+        stack_copy(peer).start()
+
+    direct = far_chips[:DIRECT]
+    for place in direct:
+        for c in range(HALVES):
+            send_stack(place * HALVES + c, summed(place * HALVES + c))
+
+    places = far_chips[len(direct) :] + [chip]
+    cuts = [0, (len(places) + 1) // 2, len(places)]
 
     def pair_copy(piece):
-        span = pl.ds(piece * share, share)
+        span = pl.ds(cuts[piece], cuts[piece + 1] - cuts[piece])
         return pltpu.make_async_remote_copy(
             src_ref=pair_out.at[span], dst_ref=pair_in.at[span],
             send_sem=pair_sems.at[0, piece], recv_sem=pair_sems.at[1, piece],
@@ -343,31 +360,23 @@
         )
 
     for piece in range(PAIR_PIECES):
-        for i in range(piece * share, (piece + 1) * share):
+        for i in range(cuts[piece], cuts[piece + 1]):
             pair_out[i] = summed(places[i] * HALVES + 1 - core)
         pair_copy(piece).start()
-
-    def stack_copy(place):
-        return pltpu.make_async_remote_copy(
-            src_ref=outgoing.at[place], dst_ref=incoming.at[chip],
-            send_sem=sems.at[6], recv_sem=sems.at[7],
-            device_id=(place * HALVES + core, now), device_id_type=MESH,
-        )
-
     for i, place in enumerate(places):
         mine_out[i] = summed(place * HALVES + core)
     stack = jnp.zeros((tiles, LANES), f32)
     for i, place in enumerate(places):
-        if i % share == 0:
-            pair_copy(i // share).wait_recv()
+        if i in cuts:
+            pair_copy(cuts.index(i)).wait_recv()
         stack = mine_out[i] + pair_in[i]
-        if i < len(far_chips):
-            outgoing[place] = stack.astype(bf16)
-            stack_copy(place).start()
-    if far_chips:
-        wait_for(incoming, len(far_chips), sems.at[7])
-    for place in far_chips:
-        stack = stack + incoming[place].astype(f32)
+        if i < len(places) - 1:
+            send_stack(place * HALVES + core, stack)
+    received = [place * HALVES + c for place in direct for c in range(HALVES)]
+    received += [place * HALVES + core for place in places[:-1]]
+    wait_for(incoming, len(received), sems.at[7])
+    for peer in received:
+        stack = stack + incoming[peer].astype(f32)
     stack_out[...] = stack
     peak_mine[...] = jnp.max(jnp.abs(stack).reshape(tiles // 8, 8, LANES), axis=0)
 
@@ -397,8 +406,7 @@
 
     for piece in range(PAIR_PIECES):
         pair_copy(piece).wait_send()
-    if far_chips:
-        wait_for(outgoing, len(far_chips), sems.at[6])
+    wait_for(outgoing, len(received), sems.at[6])
     wait_for(peak_in, n_tm - 1, sems.at[8])
 
 
@@ -439,8 +447,8 @@
             pltpu.VMEM((n_chan // HALVES, tiles, LANES), f32),
             pltpu.VMEM((n_chan // HALVES, tiles, LANES), f32),
             pltpu.VMEM((n_chan // HALVES, tiles, LANES), f32),
-            pltpu.VMEM((n_chan // HALVES, tiles, LANES), bf16),
-            pltpu.VMEM((n_chan // HALVES, tiles, LANES), bf16),
+            pltpu.VMEM((n_chan, tiles, LANES), bf16),
+            pltpu.VMEM((n_chan, tiles, LANES), bf16),
             pltpu.VMEM((8, LANES), f32),
             pltpu.VMEM((n_tm, 8, LANES), f32),
             pltpu.SemaphoreType.DMA((10,)),

time: 34.9 us -> 34.7 us (level)
  no operation moved by 1% of the time
where the time goes in v7:
time: 34.7 us; the launch traced here: 34.6 us
  Pallas kernels  32.8 us (95%)
  between operations  0.64 us (2%)
  other arithmetic  0.6 us (2%)
  local copies, waits for them, and re-layouts  0.6 us (2%)
    pallas_call x1, Pallas kernels, on_device(): pl.pallas_call(functools.partial(kernel, n_chan, n_tm, length, channels),...  32.8 us

profile of v7, /device:TPU:1, one launch (start us, length us, event | category | flops | bytes accessed | tf_op | source)
XLA Modules:
  0.0 34.6 jit_solution(11076756028069302225)
XLA Ops:
  0.6 32.8 %shard_map.59 = (f32[32,128]{1,0:T(8,128)S(1)}, f32[8,128]{1,0:T(8,128)S(1)}) custom-call(s32[32,30]{1,0:T(8,128)} %listed.1, s32[32,30]{1,0:T(8,128)} %moves.1, bf16[96,4096]{1,0:T(8,128)(2,1)} %seis.1, f32[30,1,300]{2,1,0:T(1,128)} %bitcast.4), custom_call_target="tpu_custom_call" | custom-call | tf_op jit(solution)/shard_map/pallas_call | solution.py:419
  33.4 0.6 %reduce_max.9 = f32[]{:T(128)} reduce(f32[8,128]{1,0:T(8,128)S(1)} %get-tuple-element.5, f32[]{:T(128)} %constant.0.clone.1), dimensions={0,1}, to_apply=%region_0.0 | reduce | flops 1023 | bytes 4104 | tf_op jit(solution)/shard_map/reduce_max | solution.py:462
  34.0 0.6 %copy.7 = f32[1,4096]{1,0:T(1,128)} copy(f32[1,4096]{1,0:T(1,128)S(1)} %bitcast.3) | data formatting | bytes 32768

commit v8 on v6

--- a/solution.py
+++ b/solution.py
@@ -369,7 +369,7 @@
     for place in far_chips:
         stack = stack + incoming[place].astype(f32)
     stack_out[...] = stack
-    peak_mine[...] = jnp.max(jnp.abs(stack).reshape(tiles // 8, 8, LANES), axis=0)
+    peak_mine[...] = jnp.max(jnp.abs(stack), axis=0, keepdims=True)
 
     def peak_copy(i):
         return pltpu.make_async_remote_copy(
@@ -384,7 +384,7 @@
     peak = peak_mine[...]
     for i in range(n_tm - 1):
         peak = jnp.maximum(peak, peak_in[tm_peer(i + 1)])
-    peak_out[...] = peak
+    peak_out[...] = jnp.broadcast_to(jnp.max(peak, axis=1, keepdims=True), peak_out.shape)
 
     @pl.when(now > 0)
     def _():
@@ -441,8 +441,8 @@
             pltpu.VMEM((n_chan // HALVES, tiles, LANES), f32),
             pltpu.VMEM((n_chan // HALVES, tiles, LANES), bf16),
             pltpu.VMEM((n_chan // HALVES, tiles, LANES), bf16),
-            pltpu.VMEM((8, LANES), f32),
-            pltpu.VMEM((n_tm, 8, LANES), f32),
+            pltpu.VMEM((1, LANES), f32),
+            pltpu.VMEM((n_tm, 1, LANES), f32),
             pltpu.SemaphoreType.DMA((10,)),
             pltpu.SemaphoreType.DMA((2, PAIR_PIECES)),
             pltpu.SemaphoreType.DMA((5,)),
@@ -451,7 +451,7 @@
             collective_id=0, has_side_effects=True, vmem_limit_bytes=GRANT
         ),
     )(channel_list, moveouts, seismic, jnp.transpose(waveforms, (1, 0, 2)))
-    return stack.reshape(1, piece), jnp.max(peak).reshape(1)
+    return stack.reshape(1, piece), peak[0, 0:1]
 
 
 def solution(mesh):

time: 34.9 us -> 34.7 us (level)
  other arithmetic: 0.6 us -> 0 us
  local copies, waits for them, and re-layouts: 0.6 us -> 1.12 us
    reduce_max x1 -> x0, other arithmetic: 0.6 us -> none  [on_device(): return (stack.reshape(1, piece), jnp.max(peak).reshape(1))]
    slice x0 -> x1, local copies, waits for them, and re-layouts: none -> 0.51 us  [on_device(): return (stack.reshape(1, piece), peak[0, 0:1])]
where the time goes in v8:
time: 34.7 us; the launch traced here: 34.6 us
  Pallas kernels  32.8 us (95%)
  local copies, waits for them, and re-layouts  1.12 us (3%)
  between operations  0.64 us (2%)
    pallas_call x1, Pallas kernels, on_device(): pl.pallas_call(functools.partial(kernel, n_chan, n_tm, length, channels),...  32.8 us

profile of v8, /device:TPU:1, one launch (start us, length us, event | category | flops | bytes accessed | tf_op | source)
XLA Modules:
  0.0 34.6 jit_solution(9941518743975605518)
XLA Ops:
  0.6 32.8 %shard_map.59 = (f32[32,128]{1,0:T(8,128)S(1)}, f32[8,128]{1,0:T(8,128)S(1)}) custom-call(s32[32,30]{1,0:T(8,128)} %listed.1, s32[32,30]{1,0:T(8,128)} %moves.1, bf16[96,4096]{1,0:T(8,128)(2,1)} %seis.1, f32[30,1,300]{2,1,0:T(1,128)} %bitcast.4), custom_call_target="tpu_custom_call" | custom-call | tf_op jit(solution)/shard_map/pallas_call | solution.py:411
  33.5 0.5 %slice.3 = f32[1,1]{1,0:T(1,128)} slice(f32[8,128]{1,0:T(8,128)S(1)} %get-tuple-element.5), slice={[0:1], [0:1]} | slice | bytes 8 | tf_op jit(solution)/shard_map/slice | solution.py:454
  34.0 0.6 %copy.7 = f32[1,4096]{1,0:T(1,128)} copy(f32[1,4096]{1,0:T(1,128)S(1)} %bitcast.3) | data formatting | bytes 32768

commit v9 on v7

--- a/solution.py
+++ b/solution.py
@@ -378,7 +378,7 @@
     for peer in received:
         stack = stack + incoming[peer].astype(f32)
     stack_out[...] = stack
-    peak_mine[...] = jnp.max(jnp.abs(stack).reshape(tiles // 8, 8, LANES), axis=0)
+    peak_mine[...] = jnp.max(jnp.abs(stack), axis=0, keepdims=True)
 
     def peak_copy(i):
         return pltpu.make_async_remote_copy(
@@ -393,7 +393,7 @@
     peak = peak_mine[...]
     for i in range(n_tm - 1):
         peak = jnp.maximum(peak, peak_in[tm_peer(i + 1)])
-    peak_out[...] = peak
+    peak_out[...] = jnp.broadcast_to(jnp.max(peak, axis=1, keepdims=True), peak_out.shape)
 
     @pl.when(now > 0)
     def _():
@@ -449,8 +449,8 @@
             pltpu.VMEM((n_chan // HALVES, tiles, LANES), f32),
             pltpu.VMEM((n_chan, tiles, LANES), bf16),
             pltpu.VMEM((n_chan, tiles, LANES), bf16),
-            pltpu.VMEM((8, LANES), f32),
-            pltpu.VMEM((n_tm, 8, LANES), f32),
+            pltpu.VMEM((1, LANES), f32),
+            pltpu.VMEM((n_tm, 1, LANES), f32),
             pltpu.SemaphoreType.DMA((10,)),
             pltpu.SemaphoreType.DMA((2, PAIR_PIECES)),
             pltpu.SemaphoreType.DMA((5,)),
@@ -459,7 +459,7 @@
             collective_id=0, has_side_effects=True, vmem_limit_bytes=GRANT
         ),
     )(channel_list, moveouts, seismic, jnp.transpose(waveforms, (1, 0, 2)))
-    return stack.reshape(1, piece), jnp.max(peak).reshape(1)
+    return stack.reshape(1, piece), peak[0, 0:1]
 
 
 def solution(mesh):

time: 34.7 us -> 34.6 us (level)
  other arithmetic: 0.6 us -> 0 us
  local copies, waits for them, and re-layouts: 0.6 us -> 1.12 us
    reduce_max x1 -> x0, other arithmetic: 0.6 us -> none  [on_device(): return (stack.reshape(1, piece), jnp.max(peak).reshape(1))]
    slice x0 -> x1, local copies, waits for them, and re-layouts: none -> 0.51 us  [on_device(): return (stack.reshape(1, piece), peak[0, 0:1])]
where the time goes in v9:
time: 34.6 us; the launch traced here: 34.5 us
  Pallas kernels  32.7 us (95%)
  local copies, waits for them, and re-layouts  1.12 us (3%)
  between operations  0.64 us (2%)
    pallas_call x1, Pallas kernels, on_device(): pl.pallas_call(functools.partial(kernel, n_chan, n_tm, length, channels),...  32.7 us

profile of v9, /device:TPU:1, one launch (start us, length us, event | category | flops | bytes accessed | tf_op | source)
XLA Modules:
  0.0 34.5 jit_solution(18049718100844714344)
XLA Ops:
  0.6 32.7 %shard_map.59 = (f32[32,128]{1,0:T(8,128)S(1)}, f32[8,128]{1,0:T(8,128)S(1)}) custom-call(s32[32,30]{1,0:T(8,128)} %listed.1, s32[32,30]{1,0:T(8,128)} %moves.1, bf16[96,4096]{1,0:T(8,128)(2,1)} %seis.1, f32[30,1,300]{2,1,0:T(1,128)} %bitcast.4), custom_call_target="tpu_custom_call" | custom-call | tf_op jit(solution)/shard_map/pallas_call | solution.py:419
  33.4 0.5 %slice.3 = f32[1,1]{1,0:T(1,128)} slice(f32[8,128]{1,0:T(8,128)S(1)} %get-tuple-element.5), slice={[0:1], [0:1]} | slice | bytes 8 | tf_op jit(solution)/shard_map/slice | solution.py:462
  33.9 0.6 %copy.7 = f32[1,4096]{1,0:T(1,128)} copy(f32[1,4096]{1,0:T(1,128)S(1)} %bitcast.3) | data formatting | bytes 32768

commit v10 on v6

--- a/solution.py
+++ b/solution.py
@@ -309,16 +309,19 @@
 
     def correlate(group, total):
         numers = []
-        for p in range(at_once * PER // 2):
-            pair = group * (at_once * PER // 2) + p
-            both = lax.dot_general(
-                lhs[pair], jnp.concatenate([toeplitz_of(pair * 2), toeplitz_of(pair * 2 + 1)], axis=0),
+        for p in range(at_once * PER // 4):
+            quad = group * (at_once * PER // 4) + p
+            wide = lax.dot_general(
+                lhs[pl.ds(quad * 2, 2)].reshape(8 * tiles, WAVE_BLOCKS * LANES),
+                jnp.concatenate([toeplitz_of(quad * 4 + i) for i in range(4)], axis=0),
                 (((1,), (1,)), ((), ())), preferred_element_type=f32,
             )
-            first, second, third, fourth = (both[i * tiles : (i + 1) * tiles] for i in range(4))
-            swapped = pltpu.roll(jnp.where(left_all, second, third), HALF_LANES, 1)
-            numers.append(jnp.where(left_all, first, swapped))
-            numers.append(jnp.where(left_all, swapped, fourth))
+            for h in range(2):
+                both = wide[h * 4 * tiles : (h + 1) * 4 * tiles, h * LANES : (h + 1) * LANES]
+                first, second, third, fourth = (both[i * tiles : (i + 1) * tiles] for i in range(4))
+                swapped = pltpu.roll(jnp.where(left_all, second, third), HALF_LANES, 1)
+                numers.append(jnp.where(left_all, first, swapped))
+                numers.append(jnp.where(left_all, swapped, fourth))
         for u in range(at_once):
             station = group * at_once + u
             for d in range(PER):

time: 34.9 us -> 34.8 us (level)
  no operation moved by 1% of the time
where the time goes in v10:
time: 34.8 us; the launch traced here: 34.7 us
  Pallas kernels  32.9 us (95%)
  between operations  0.64 us (2%)
  other arithmetic  0.6 us (2%)
  local copies, waits for them, and re-layouts  0.6 us (2%)
    pallas_call x1, Pallas kernels, on_device(): pl.pallas_call(functools.partial(kernel, n_chan, n_tm, length, channels),...  32.9 us

profile of v10, /device:TPU:1, one launch (start us, length us, event | category | flops | bytes accessed | tf_op | source)
XLA Modules:
  0.0 34.7 jit_solution(2533377886766033578)
XLA Ops:
  0.6 32.9 %shard_map.59 = (f32[32,128]{1,0:T(8,128)S(1)}, f32[8,128]{1,0:T(8,128)S(1)}) custom-call(s32[32,30]{1,0:T(8,128)} %listed.1, s32[32,30]{1,0:T(8,128)} %moves.1, bf16[96,4096]{1,0:T(8,128)(2,1)} %seis.1, f32[30,1,300]{2,1,0:T(1,128)} %bitcast.4), custom_call_target="tpu_custom_call" | custom-call | tf_op jit(solution)/shard_map/pallas_call | solution.py:414
  33.5 0.6 %reduce_max.9 = f32[]{:T(128)} reduce(f32[8,128]{1,0:T(8,128)S(1)} %get-tuple-element.5, f32[]{:T(128)} %constant.0.clone.1), dimensions={0,1}, to_apply=%region_0.0 | reduce | flops 1023 | bytes 4104 | tf_op jit(solution)/shard_map/reduce_max | solution.py:457
  34.1 0.6 %copy.7 = f32[1,4096]{1,0:T(1,128)} copy(f32[1,4096]{1,0:T(1,128)S(1)} %bitcast.3) | data formatting | bytes 32768
